TPU v7x, 32 devices: a whole 2x2x4 slice. The times are simulated.
32 devices in a mesh: dom: 4 (over z), bulk: 8 (over y, x, core).
Axes of the slice: x: 2, y: 2, z: 4, core: 2. Of those that a mesh axis runs over, the one named last changes fastest.
Arguments:
- node_patch: int32 [524288], P(('dom', 'bulk')), may hold values from 0 to 19999, as said below
- node_span: int32 [524288], P(('dom', 'bulk')), may hold values from 0 to 15
- start_grid: int32 [2, 524288], P(None, ('dom', 'bulk')), may hold values from 0 to 15
- target: float32 [3, 524288], P(None, ('dom', 'bulk')), may hold values from -0.1 to 1.1
- net: float32 [20000, 1024], P('bulk'), as said below
Outputs:
- placed: float32 [9, 524288], P(None, ('dom', 'bulk'))
Inputs may be any that keep to these rules, and one draw needn't show every extreme that they name: In each partition's block of 16384 nodes (block k of the array, dom slowest), no owner node_patch // 2500 is named by more than 2560 nodes, and one owner is named by exactly 2560; that owner is the same for all blocks of one index of dom. `net`: component 3 (the weight) of every control point is positive.
All inputs are finite; a program needn't handle non-finite values.
Results may differ from a plain program's by a relative error of at most 0.0003.
Values sent between devices are 32-bit elements; how exact they have to be, the bound alone decides.
No kernel may reach another device: no remote copies, remote signals or barrier semaphores. Data moves between devices by JAX's collectives and lax.ppermute only.
A program may use at most 128 MiB of HBM per device.

v0:
```python
import jax
import jax.numpy as jnp
from jax import lax
from jax.sharding import PartitionSpec as P

SPANS = 16
LEVELS = 16
ITERS = 4


damping = 0.1
highest = lax.Precision.HIGHEST


def bernstein(param):
    other = 1.0 - param
    value = jnp.stack(
        [
            other * other * other,
            3.0 * param * other * other,
            3.0 * param * param * other,
            param * param * param,
        ]
    )
    slope = jnp.stack(
        [
            -3.0 * other * other,
            3.0 * other * other - 6.0 * param * other,
            6.0 * param * other - 3.0 * param * param,
            3.0 * param * param,
        ]
    )
    return (value, slope)


def surface(control, upar, vpar):
    base_u, slope_u = bernstein(upar)
    basis_along_vdir, slope_vdir = bernstein(vpar)
    mixed_partial = jnp.sum(base_u[None, :, None, :] * control, axis=1)
    mixed_partial_udir = jnp.sum(slope_u[None, :, None, :] * control, axis=1)
    homogeneous_point = jnp.sum(basis_along_vdir[None] * mixed_partial, axis=1)
    homogeneous_udiff = jnp.sum(basis_along_vdir[None] * mixed_partial_udir, axis=1)
    homogeneous_vdiff = jnp.sum(slope_vdir[None] * mixed_partial, axis=1)
    rational_weight = homogeneous_point[3]
    surface_point = homogeneous_point[:3] / rational_weight
    tangent_udir = (homogeneous_udiff[:3] - surface_point * homogeneous_udiff[3]) / rational_weight
    tangent_vdir = (homogeneous_vdiff[:3] - surface_point * homogeneous_vdiff[3]) / rational_weight
    return (surface_point, tangent_udir, tangent_vdir)


def project(coeffs, goal, start):
    control = coeffs.reshape(4, 4, 4, -1)
    upar = start[0]
    vpar = start[1]
    for step in range(ITERS):
        surface_point, tangent_udir, tangent_vdir = surface(control, upar, vpar)
        miss = surface_point - goal
        grad_u = jnp.sum(tangent_udir * miss, axis=0)
        grad_v = jnp.sum(tangent_vdir * miss, axis=0)
        h_uu = jnp.sum(tangent_udir * tangent_udir, axis=0) + damping
        h_vv = jnp.sum(tangent_vdir * tangent_vdir, axis=0) + damping
        h_uv = jnp.sum(tangent_udir * tangent_vdir, axis=0)
        determ = h_uu * h_vv - h_uv * h_uv
        upar = jnp.clip(upar - (h_vv * grad_u - h_uv * grad_v) / determ, 0.0, 1.0)
        vpar = jnp.clip(vpar - (h_uu * grad_v - h_uv * grad_u) / determ, 0.0, 1.0)
    surface_point, tangent_udir, tangent_vdir = surface(control, upar, vpar)
    return jnp.concatenate([surface_point, tangent_udir, tangent_vdir], axis=0)


def rank_within(byowner):
    nodes, owners = byowner.shape
    block = min(512, nodes)
    count = nodes // block
    grouped = byowner.reshape(count, block, owners)
    lower = (jnp.arange(block)[:, None] > jnp.arange(block)[None, :]).astype(jnp.float32)
    inner = jnp.einsum("ij,bjo->bio", lower, grouped, precision=highest)
    totals = jnp.sum(grouped, axis=1)
    offsets = jnp.cumsum(totals, axis=0) - totals
    before = (inner + offsets[:, None, :]).reshape(nodes, owners)
    return jnp.sum(before * byowner, axis=1)


def to_slots(values, byowner, byslot):
    masked = values[:, None, :] * byowner.T[None, :, :]
    rows, owners, nodes = masked.shape
    placed = jnp.dot(masked.reshape(rows * owners, nodes), byslot, precision=highest)
    return placed.reshape(rows, owners, -1)


def from_slots(slotted, byowner, byslot):
    rows, owners, capacity = slotted.shape
    spread = jnp.dot(slotted.reshape(rows * owners, capacity), byslot.T, precision=highest)
    spread = spread.reshape(rows, owners, -1)
    return jnp.sum(spread * byowner.T[None, :, :], axis=1)


def body(node_patch, node_span, start_grid, target, net):
    owners = lax.axis_size("bulk")
    patch_dev = net.shape[0]
    nodes = node_patch.shape[0]
    capacity = nodes * 5 // 32
    owner = node_patch // patch_dev
    local_row = (node_patch - owner * patch_dev) * SPANS + node_span
    byowner = (owner[:, None] == jnp.arange(owners, dtype=jnp.int32)[None, :]).astype(jnp.float32)
    within = rank_within(byowner).astype(jnp.int32)
    byslot = (within[:, None] == jnp.arange(capacity, dtype=jnp.int32)[None, :]).astype(jnp.float32)
    net_rows = net.reshape(-1, 64)
    start = (start_grid.astype(jnp.float32) + 0.5) / LEVELS
    payload = jnp.concatenate([target, start, local_row.astype(jnp.float32)[None]], axis=0)
    outgoing = to_slots(payload, byowner, byslot)
    received = lax.all_to_all(outgoing, "bulk", split_axis=1, concat_axis=1, tiled=True)
    count = received.shape[2]
    rows = received[5].astype(jnp.int32).reshape(-1)
    coeffs = net_rows[rows].T
    result = project(coeffs, received[0:3].reshape(3, -1), received[3:5].reshape(2, -1))
    answered = lax.all_to_all(
        result.reshape(9, owners, count), "bulk", split_axis=1, concat_axis=1, tiled=True
    )
    return from_slots(answered, byowner, byslot)


def solution(mesh):
    return jax.shard_map(
        body,
        mesh=mesh,
        in_specs=(
            P(("dom", "bulk")),
            P(("dom", "bulk")),
            P(None, ("dom", "bulk")),
            P(None, ("dom", "bulk")),
            P("bulk", None),
        ),
        out_specs=P(None, ("dom", "bulk")),
        check_vma=False,
    )
```

profile of v0, /device:TPU:0, one launch (start us, length us, event | category | flops | bytes accessed | tf_op | source)
XLA Modules:
  0.0 343.7 jit_solution(15414015366005871723)
XLA Ops:
  0.0 0.9 add_convert_fusion
  1.2 0.5 fusion.18
  2.4 64.8 %fusion.3 = f32[6,8,2560]{2,1,0:T(8,128)S(1)} fusion(s32[16384]{0:T(1024)S(1)} %bitcast.100, f32[6,8,16384]{2,1,0:T(8,128)S(1)} %fusion.72), kind=kOutput, calls=%fused_computation.4 | convolution fusion | flops 24201134080 | bytes 3702784 | tf_op jit(solution)/shard_map/dot_general | solution.py:86
  67.2 1.1 copy.24
  68.3 5.2 %all-to-all-start = ((f32[6,8,2560]{2,0,1:T(8,128)}), f32[6,8,2560]{2,0,1:T(8,128)S(1)}, u32[]{:S(2)}, u32[]{:S(2)}) async-start(f32[6,8,2560]{2,0,1:T(8,128)} %copy.24), calls=%async_computation | async-start | bytes 1310720 | tf_op jit(solution)/shard_map/all_to_all | solution.py:111
  73.5 16.0 %reshape.4551 = f32[40000,64]{1,0:T(8,128)} reshape(f32[2500,1024]{1,0:T(8,128)} %param.9) | data formatting | bytes 20480000 | tf_op jit(solution)/shard_map/reshape | solution.py:107
  89.8 74.9 %gather_fusion = f32[20480,64]{1,0:T(8,128)} fusion(f32[40000,64]{1,0:T(8,128)} %reshape.4551, s32[20480]{0:T(1024)S(1)} %broadcast_clamp_fusion), kind=kCustom, calls=%fused_computation | custom fusion | bytes 10567680 | tf_op jit(solution)/shard_map/gather | solution.py:114
  164.7 9.1 %copy.25 = f32[64,20480]{1,0:T(8,128)} copy(f32[64,20480]{0,1:T(8,128)} %bitcast.59) | data formatting | bytes 10485760 | tf_op jit(solution)/shard_map/transpose | solution.py:114
  173.8 6.1 %reshape.4552 = f32[4,4,4,20480]{3,2,1,0:T(4,128)} reshape(f32[64,20480]{1,0:T(8,128)} %copy.25) | data formatting | bytes 10485760 | tf_op jit(solution)/shard_map/reshape | solution.py:52
  179.9 0.4 multiply_multiply_fusion.46
  180.3 0.4 multiply_multiply_fusion.49
  180.8 0.6 pad_maximum_fusion.3
  181.4 6.0 %multiply_reduce_fusion.8 = (f32[4,4,20480]{2,1,0:T(4,128)S(1)}, f32[4,4,20480]{2,1,0:T(4,128)S(1)}) fusion(f32[4,4,4,20480]{3,2,1,0:T(4,128)} %reshape.4552, f32[4,20480]{1,0:T(4,128)S(1)} %get-tuple-element.163, f32[4,20480]{1,0:T(4,128)S(1)} %get-tuple-element.162), kind=kLoop, calls=%fused_computation.16 | loop fusion | flops 4587520 | bytes 8519680 | tf_op jit(solution)/shard_map/reduce_sum | solution.py:39
  187.4 0.6 pad_maximum_fusion.2
  188.0 2.7 multiply_reduce_fusion.22
  191.3 1.1 multiply_reduce_fusion.41
  192.7 0.3 fusion.36
  193.2 0.3 multiply_multiply_fusion.38
  193.5 0.3 pad_maximum_fusion.8
  193.8 0.7 pad_maximum_fusion.7
  194.6 2.7 multiply_reduce_fusion.6
  197.3 0.3 pad_maximum_fusion.9
  197.7 0.3 pad_maximum_fusion.6
  198.0 2.7 multiply_reduce_fusion.19
  201.2 1.1 multiply_reduce_fusion.36
  202.6 0.3 fusion.38
  203.1 0.3 multiply_multiply_fusion.28
  203.7 0.3 pad_maximum_fusion.11
  204.1 2.9 multiply_reduce_fusion.4
  207.3 0.3 pad_maximum_fusion.10
  207.6 2.7 multiply_reduce_fusion.16
  210.8 1.1 multiply_reduce_fusion.31
  212.2 0.3 fusion.40
  212.7 0.3 multiply_multiply_fusion.18
  213.1 0.3 pad_maximum_fusion.16
  213.7 2.7 multiply_reduce_fusion.2
  216.5 0.3 pad_maximum_fusion.17
  217.1 2.9 multiply_reduce_fusion.13
  220.5 1.1 multiply_reduce_fusion.26
  221.9 0.3 multiply_multiply_fusion.5
  222.4 0.3 fusion.43
  223.4 2.7 multiply_reduce_fusion
  226.8 2.7 multiply_reduce_fusion.12
  230.0 0.6 pad_maximum_fusion
  230.6 0.8 copy.29
  231.4 0.5 copy.26
  231.9 22.2 %all_to_all.10 = f32[9,8,2560]{2,0,1:T(8,128)S(1)} all-to-all(f32[9,8,2560]{2,0,1:T(8,128)S(1)} %copy.26), channel_id=1, replica_groups=mesh['dom'=4,'bulk'=8] {'bulk'}, dimensions={1} | all-to-all | bytes 1474560 | tf_op jit(solution)/shard_map/all_to_all | solution.py:116
  254.0 89.2 %fusion.11 = f32[9,16384]{1,0:T(8,128)} fusion(f32[8,16384]{1,0:T(8,128)S(1)} %fusion.22, s32[16384]{0:T(1024)S(1)} %bitcast.101, f32[9,8,2560]{2,0,1:T(8,128)S(1)} %all_to_all.10), kind=kOutput, calls=%fused_computation.19 | convolution fusion | flops 36282941440 | bytes 1916928 | tf_op jit(solution)/shard_map/dot_general | solution.py:92
  (65 shorter events, 7.8 us)
Async XLA Ops:
  0.9 0.9 copy-start.1
  0.9 1.0 copy-start
  68.3 21.2 %all-to-all-start = ((f32[6,8,2560]{2,0,1:T(8,128)}), f32[6,8,2560]{2,0,1:T(8,128)S(1)}, u32[]{:S(2)}, u32[]{:S(2)}) async-start(f32[6,8,2560]{2,0,1:T(8,128)} %copy.24), calls=%async_computation | async-start | bytes 1310720 | tf_op jit(solution)/shard_map/all_to_all | solution.py:111
  188.0 6.6 %slice-start = ((s8[5242880]{0:T(1024)(128)(4,1)}), s8[4194304]{0:T(1024)(128)(4,1)S(1)}, s32[]{:S(2)}) async-start(s8[5242880]{0:T(1024)(128)(4,1)} %bitcast.57), calls=%async_computation.2 | async-start | bytes 8388608
  191.0 3.6 %slice-start.1 = ((s8[5242880]{0:T(1024)(128)(4,1)}), s8[1048576]{0:T(1024)(128)(4,1)S(1)}, s32[]{:S(2)}) async-start(s8[5242880]{0:T(1024)(128)(4,1)} %bitcast.57), calls=%async_computation.3 | async-start | bytes 2097152
where the time goes:
time: 350 us; the launch traced here: 344 us
  matrix products  154 us (44%)
  local copies, waits for them, and re-layouts  110 us (31%)
  other arithmetic  50.7 us (14%)
  blocking collectives  22.2 us (6%)
  starting transfers between devices  5.17 us (1%)
    dot_general x1, matrix products, from_slots(): jnp.dot(slotted.reshape(rows * owners, capacity), byslot.T, precision=hig...  89.2 us
    gather x1, local copies, waits for them, and re-layouts, body(): coeffs = net_rows[rows].T  74.9 us
    dot_general x1, matrix products, to_slots(): jnp.dot(masked.reshape(rows * owners, nodes), byslot, precision=highest)  64.8 us
    all_to_all x1, blocking collectives, body(): lax.all_to_all(result.reshape(9, owners, count), 'bulk', split_axis=1, co...  22.2 us
    reshape x1, local copies, waits for them, and re-layouts, body(): net_rows = net.reshape(-1, 64)  16 us
    reduce_sum x4, other arithmetic, surface(): mixed_partial = jnp.sum(base_u[None, :, None, :] * control, axis=1)  14.4 us
    reduce_sum x4, other arithmetic, surface(): homogeneous_vdiff = jnp.sum(slope_vdir[None] * mixed_partial, axis=1)  10.9 us
    transpose x1, local copies, waits for them, and re-layouts, body(): coeffs = net_rows[rows].T  9.06 us
  transfers between devices with their start and end apart: 1, of which 0 were waited for; matrix products, arithmetic and copies ran while one was open for 5% of the time, Pallas kernels for 0%

commit v1 on v0

v1 whole, which is shorter than its diff:
```python
import functools

import jax
import jax.numpy as jnp
from jax import lax
from jax.experimental import pallas as pl
from jax.experimental.pallas import tpu as pltpu
from jax.sharding import PartitionSpec as P

SPANS = 16
LEVELS = 16
ITERS = 4
LANES = 128
SENT = 6
GIVEN = 9

damping = 0.1


def round_up(value, unit):
    return -(-value // unit) * unit


def iota(shape, dim):
    return lax.broadcasted_iota(jnp.int32, shape, dim)


def route_kernel(owners, windows, patch_dev, patch_pad, patch_ref, span_ref, grid_ref, target_ref,
                 sent_ref, key_ref, first_ref, code_ref, load_ref, slot_ref, first_smem, sem):
    blocks = patch_ref.shape[0]
    patch = patch_ref[...]
    owner = jnp.zeros_like(patch)
    for o in range(1, owners):
        owner += (patch >= o * patch_dev).astype(jnp.int32)
    span = span_ref[...]
    row = 2 * ((span >> 1) * patch_pad + patch - owner * patch_dev) + (span & 1)

    lane = iota((LANES, LANES), 1)
    sub = iota((LANES, LANES), 0)
    upto = (sub <= lane).astype(jnp.bfloat16)
    every = jnp.ones((LANES, LANES), jnp.bfloat16)
    counter = jnp.concatenate([upto, every], axis=1)
    earlier = (iota((blocks, blocks), 1) < iota((blocks, blocks), 0)).astype(jnp.bfloat16)
    blane = iota((blocks, LANES), 1)
    diagonal = iota((blocks, blocks), 0) == iota((blocks, blocks), 1)

    within = jnp.zeros_like(patch)
    for o in range(owners):
        mine = owner == o
        mask = mine.astype(jnp.bfloat16)
        counts = jnp.dot(mask, counter, preferred_element_type=jnp.float32)
        total = counts[:, LANES:]
        offset = jnp.dot(earlier, total.astype(jnp.bfloat16), preferred_element_type=jnp.float32).astype(jnp.int32)
        before = counts[:, :LANES].astype(jnp.int32) - mine.astype(jnp.int32)
        total = total.astype(jnp.int32)
        within = jnp.where(mine, before + offset, within)
        first = jnp.sum(jnp.where(diagonal, offset.astype(jnp.float32), 0.0), axis=0, keepdims=True)
        first_ref[o:o + 1, :] = first.astype(jnp.int32) >> 7
        word = jnp.where(mine, blane + LANES * (blane - before), 0)
        for bit in range(7):
            moves = 1 << (7 + bit)
            coming = pltpu.roll(word, LANES - (1 << bit), 1)
            word = jnp.where((coming & moves) != 0, coming, jnp.where((word & moves) != 0, 0, word))
        edge = offset & (LANES - 1)
        rank = (blane - edge) & (LANES - 1)
        source = jnp.take_along_axis(word & (LANES - 1), rank, axis=1)
        valid = rank < total
        code = source + jnp.where(valid, jnp.where(blane >= edge, 128, 256), 0)
        code_ref[o * blocks:(o + 1) * blocks, :] = code

    key_ref[...] = (owner * (windows + 1) * LANES) + within
    copy = pltpu.make_async_copy(first_ref, first_smem, sem)
    copy.start()

    slot_ref[...] = jnp.zeros_like(slot_ref)
    rowf = row.astype(jnp.float32)
    load_ref[...] = jnp.zeros_like(load_ref)
    for b in range(blocks):
        load_ref[8 * b:8 * b + 3, :] = target_ref[:, b * LANES:(b + 1) * LANES]
        load_ref[8 * b + 3:8 * b + 5, :] = (grid_ref[:, b * LANES:(b + 1) * LANES].astype(jnp.float32) + 0.5) * (1.0 / LEVELS)
        load_ref[8 * b + 5:8 * b + 6, :] = rowf[b:b + 1, :]
    copy.wait()

    def place(b, carry):
        load = load_ref[pl.ds(pl.multiple_of(8 * b, 8), 8), :]
        for o in range(owners):
            code = jnp.broadcast_to(code_ref[pl.ds(o * blocks + b, 1), :], (8, LANES))
            moved = jnp.take_along_axis(load, code & (LANES - 1), axis=1)
            base = pl.multiple_of((o * (windows + 1) + first_smem[o, b]) * 8, 8)
            pltpu.store(slot_ref.at[pl.ds(base, 8), :], moved, mask=(code & 128) != 0)
            pltpu.store(slot_ref.at[pl.ds(base + 8, 8), :], moved, mask=(code & 256) != 0)
        return carry

    lax.fori_loop(0, blocks, place, 0)

    for o in range(owners):
        for c in range(SENT):
            for w in range(0, windows, 8):
                size = min(8, windows - w)
                rows = slot_ref[pl.ds((o * (windows + 1) + w) * 8 + c, size, stride=8), :]
                sent_ref[o, c * windows + w:c * windows + w + size, :] = rows


def route(node_patch, node_span, start_grid, target, owners, windows, patch_dev, patch_pad):
    nodes = node_patch.shape[0]
    blocks = nodes // LANES
    return pl.pallas_call(
        functools.partial(route_kernel, owners, windows, patch_dev, patch_pad),
        out_shape=(
            jax.ShapeDtypeStruct((owners, SENT * windows, LANES), jnp.float32),
            jax.ShapeDtypeStruct((blocks, LANES), jnp.int32),
            jax.ShapeDtypeStruct((owners, blocks), jnp.int32),
        ),
        in_specs=[pl.BlockSpec(memory_space=pltpu.VMEM)] * 4,
        out_specs=[pl.BlockSpec(memory_space=pltpu.VMEM)] * 3,
        scratch_shapes=[
            pltpu.VMEM((owners * blocks, LANES), jnp.int32),
            pltpu.VMEM((8 * blocks, LANES), jnp.float32),
            pltpu.VMEM((owners * (windows + 1) * 8, LANES), jnp.float32),
            pltpu.SMEM((owners, blocks), jnp.int32),
            pltpu.SemaphoreType.DMA,
        ],
        compiler_params=pltpu.CompilerParams(vmem_limit_bytes=40 * 2**20),
        name="route",
    )(node_patch.reshape(blocks, LANES), node_span.reshape(blocks, LANES), start_grid, target)


def bernstein(param):
    other = 1.0 - param
    square, cross, low = other * other, param * other, param * param
    value = (other * square, 3.0 * cross * other, 3.0 * param * cross, param * low)
    slope = (-3.0 * square, 3.0 * square - 6.0 * cross, 6.0 * cross - 3.0 * low, 3.0 * low)
    return value, slope


def weighted(weights, values):
    return (weights[0] * values[0] + weights[1] * values[1]) + (weights[2] * values[2] + weights[3] * values[3])


def surface(read, upar, vpar):
    base_u, slope_u = bernstein(upar)
    base_v, slope_v = bernstein(vpar)
    point, along_u, along_v = [], [], []
    for c in range(4):
        mixed, mixed_u = [], []
        for j in range(4):
            column = [read(c * 16 + i * 4 + j) for i in range(4)]
            mixed.append(weighted(base_u, column))
            mixed_u.append(weighted(slope_u, column))
        point.append(weighted(base_v, mixed))
        along_u.append(weighted(base_v, mixed_u))
        along_v.append(weighted(slope_v, mixed))
    inverse = 1.0 / point[3]
    position = [point[c] * inverse for c in range(3)]
    tangent_u = [(along_u[c] - position[c] * along_u[3]) * inverse for c in range(3)]
    tangent_v = [(along_v[c] - position[c] * along_v[3]) * inverse for c in range(3)]
    return position, tangent_u, tangent_v


def inner(left, right):
    return left[0] * right[0] + left[1] * right[1] + left[2] * right[2]


def project(read, goal, upar, vpar):
    for _ in range(ITERS):
        position, tangent_u, tangent_v = surface(read, upar, vpar)
        miss = [position[c] - goal[c] for c in range(3)]
        grad_u = inner(tangent_u, miss)
        grad_v = inner(tangent_v, miss)
        h_uu = inner(tangent_u, tangent_u) + damping
        h_vv = inner(tangent_v, tangent_v) + damping
        h_uv = inner(tangent_u, tangent_v)
        inverse = 1.0 / (h_uu * h_vv - h_uv * h_uv)
        upar = jnp.clip(upar - (h_vv * grad_u - h_uv * grad_v) * inverse, 0.0, 1.0)
        vpar = jnp.clip(vpar - (h_uu * grad_v - h_uv * grad_u) * inverse, 0.0, 1.0)
    position, tangent_u, tangent_v = surface(read, upar, vpar)
    return position + tangent_u + tangent_v


def project_kernel(sources, windows, given_pad, got_ref, net_ref, out_ref,
                   net_vmem, index_ref, index_smem, tile_ref, coeff_ref, net_sem, index_sem):
    patches = net_ref.shape[0]
    chunks = net_ref.shape[1] // LANES
    patch_pad = net_vmem.shape[0] // chunks
    groups = sources // 8
    sent = SENT * windows
    loads = []
    for c in range(chunks):
        loads.append(pltpu.make_async_copy(
            net_ref.at[:, pl.ds(c * LANES, LANES)], net_vmem.at[pl.ds(c * patch_pad, patches), :], net_sem.at[c]))
        loads[-1].start()

    def arrived(g, c, w):
        return got_ref[pl.ds(g * 8 * sent + c * windows + w, 8, stride=sent), :]

    for w in range(windows):
        for g in range(groups):
            code = arrived(g, 5, w).astype(jnp.int32)
            index_ref[pl.ds((w * groups + g) * 8, 8), :] = code >> 1
    copy = pltpu.make_async_copy(index_ref, index_smem, index_sem)
    copy.start()
    copy.wait()
    for load in loads:
        load.wait()

    def group_step(t, carry):
        w = t // groups
        g = t - w * groups
        code = arrived(g, 5, w).astype(jnp.int32)
        odd = (code & 1) == 1
        for s in range(8):
            for i in range(LANES):
                at = index_smem[t * 8 + s, i]
                tile_ref[s * LANES + i:s * LANES + i + 1, :] = net_vmem[pl.ds(at, 1), :]
            both = tile_ref[s * LANES:(s + 1) * LANES, :].T
            picked = jnp.where(odd[s:s + 1, :], both[64:, :], both[:64, :])
            coeff_ref[pl.ds(s, 64, stride=8), :] = picked

        def read(k):
            return coeff_ref[8 * k:8 * k + 8, :]

        goal = [arrived(g, c, w) for c in range(3)]
        result = project(read, goal, arrived(g, 3, w), arrived(g, 4, w))
        for c in range(GIVEN):
            out_ref[pl.ds(g * 8 * given_pad + c * windows + w, 8, stride=given_pad), :] = result[c]
        return carry

    lax.fori_loop(0, windows * groups, group_step, 0)


def project_nodes(got, net, windows, patch_pad, given_pad):
    sources = got.shape[0]
    chunks = net.shape[1] // LANES
    tiles = windows * sources
    return pl.pallas_call(
        functools.partial(project_kernel, sources, windows, given_pad),
        out_shape=jax.ShapeDtypeStruct((sources * given_pad, LANES), jnp.float32),
        in_specs=[pl.BlockSpec(memory_space=pltpu.VMEM), pl.BlockSpec(memory_space=pl.ANY)],
        out_specs=pl.BlockSpec(memory_space=pltpu.VMEM),
        scratch_shapes=[
            pltpu.VMEM((chunks * patch_pad, LANES), jnp.float32),
            pltpu.VMEM((tiles, LANES), jnp.int32),
            pltpu.SMEM((tiles, LANES), jnp.int32),
            pltpu.VMEM((8 * LANES, LANES), jnp.float32),
            pltpu.VMEM((64 * 8, LANES), jnp.float32),
            pltpu.SemaphoreType.DMA((chunks,)),
            pltpu.SemaphoreType.DMA,
        ],
        compiler_params=pltpu.CompilerParams(vmem_limit_bytes=40 * 2**20),
        name="project",
    )(got.reshape(sources * SENT * windows, LANES), net)


def return_kernel(owners, windows, given_pad, key_ref, first_smem, got_ref, out_ref):
    blocks = key_ref.shape[0]
    sub = iota((8, LANES), 0)

    def fetch(b, carry):
        key = jnp.broadcast_to(key_ref[pl.ds(b, 1), :], (8, LANES))
        lane = key & (LANES - 1)
        key = key >> 7
        rest = key - sub
        main = jnp.zeros((8, LANES), jnp.float32)
        last = jnp.zeros((8, LANES), jnp.float32)
        for o in range(owners):
            w = first_smem[o, b]
            for step in range(2):
                at = jnp.minimum(w + step, windows - 1)
                rows = got_ref[pl.ds(o * given_pad + at, 8, stride=windows), :]
                moved = jnp.take_along_axis(rows, lane, axis=1)
                main = jnp.where(key == o * (windows + 1) + at, moved, main)
            at = jnp.minimum(w, windows - 8)
            rows = got_ref[pl.ds(o * given_pad + 8 * windows + at, 8), :]
            moved = jnp.take_along_axis(rows, lane, axis=1)
            last = jnp.where(rest == o * (windows + 1) + at, moved, last)
        at = pl.ds(pl.multiple_of(b * LANES, LANES), LANES)
        out_ref[0:8, at] = main
        out_ref[8:9, at] = jnp.sum(last, axis=0, keepdims=True)
        return carry

    lax.fori_loop(0, blocks, fetch, 0)


def return_nodes(key, first, got, windows, given_pad):
    owners, blocks = first.shape
    return pl.pallas_call(
        functools.partial(return_kernel, owners, windows, given_pad),
        out_shape=jax.ShapeDtypeStruct((GIVEN, blocks * LANES), jnp.float32),
        in_specs=[
            pl.BlockSpec(memory_space=pltpu.VMEM),
            pl.BlockSpec(memory_space=pltpu.SMEM),
            pl.BlockSpec(memory_space=pltpu.VMEM),
        ],
        out_specs=pl.BlockSpec(memory_space=pltpu.VMEM),
        compiler_params=pltpu.CompilerParams(vmem_limit_bytes=40 * 2**20),
        name="give_back",
    )(key, first, got.reshape(owners * given_pad, LANES))


def body(node_patch, node_span, start_grid, target, net):
    owners = lax.axis_size("bulk")
    patch_dev = net.shape[0]
    patch_pad = round_up(patch_dev, 8)
    nodes = node_patch.shape[0]
    windows = nodes * 5 // 32 // LANES
    given_pad = round_up(GIVEN * windows, 8)
    sent, key, first = route(node_patch, node_span, start_grid, target, owners, windows, patch_dev, patch_pad)
    got = lax.all_to_all(sent, "bulk", split_axis=0, concat_axis=0, tiled=True)
    placed = project_nodes(got, net, windows, patch_pad, given_pad)
    answered = lax.all_to_all(
        placed.reshape(owners, given_pad, LANES), "bulk", split_axis=0, concat_axis=0, tiled=True)
    return return_nodes(key, first, answered, windows, given_pad)


def solution(mesh):
    return jax.shard_map(
        body,
        mesh=mesh,
        in_specs=(
            P(("dom", "bulk")),
            P(("dom", "bulk")),
            P(None, ("dom", "bulk")),
            P(None, ("dom", "bulk")),
            P("bulk", None),
        ),
        out_specs=P(None, ("dom", "bulk")),
        check_vma=False,
    )
```

time: 350 us -> 97.8 us (0.28); the launches traced: 344 us -> 97.4 us
  matrix products: 154 us -> 0 us
  local copies, waits for them, and re-layouts: 110 us -> 7.44 us
  Pallas kernels: 0 us -> 61 us
  other arithmetic: 50.7 us -> 0 us
  blocking collectives: 22.2 us -> 29 us
  starting transfers between devices: 5.17 us -> 0 us
    dot_general x3 -> x0, matrix products: 154 us -> none  [the longest x1 89.2 us: from_slots(): jnp.dot(slotted.reshape(rows * owners, capacity), byslot.T, precision=hig...]
    gather x1 -> x0, local copies, waits for them, and re-layouts: 74.9 us -> none  [body(): coeffs = net_rows[rows].T]
    pallas_call x0 -> x3, Pallas kernels: none -> 61 us  [the longest x1 32.4 us: project_nodes(): pl.pallas_call(functools.partial(project_kernel, sources, windows, given_...]
    reduce_sum x15 -> x0, other arithmetic: 35.4 us -> none  [the longest x4 14.4 us: surface(): mixed_partial = jnp.sum(base_u[None, :, None, :] * control, axis=1)]
    reshape x4 -> x0, local copies, waits for them, and re-layouts: 22.6 us -> none  [the longest x1 16 us: body(): net_rows = net.reshape(-1, 64)]
    transpose x1 -> x0, local copies, waits for them, and re-layouts: 9.06 us -> none  [body(): coeffs = net_rows[rows].T]
    all_to_all x1 -> x2, blocking collectives: 22.2 us -> 29 us  [the longest x1 14.6 us: body(): lax.all_to_all(placed.reshape(owners, given_pad, LANES), 'bulk', split_ax...]
    another operation x19 -> x0, other arithmetic: 6.73 us -> none  [the longest x9 3.54 us: bernstein(): jnp.stack([-3.0 * other * other, 3.0 * other * other - 6.0 * param * othe...]
  transfers between devices with their start and end apart: 1 -> 0, of which waited for: 0 -> 0; matrix products, arithmetic and copies ran while one was open for 5% -> 0% of each run, Pallas kernels for 0% -> 0%
where the time goes in v1:
time: 97.8 us; the launch traced here: 97.4 us
  Pallas kernels  61 us (62%)
  blocking collectives  29 us (30%)
  local copies, waits for them, and re-layouts  7.44 us (8%)
    pallas_call x1, Pallas kernels, project_nodes(): pl.pallas_call(functools.partial(project_kernel, sources, windows, given_...  32.4 us
    all_to_all x1, blocking collectives, body(): lax.all_to_all(placed.reshape(owners, given_pad, LANES), 'bulk', split_ax...  14.6 us
    pallas_call x1, Pallas kernels, route(): pl.pallas_call(functools.partial(route_kernel, owners, windows, patch_dev...  14.4 us
    all_to_all x1, blocking collectives, body(): got = lax.all_to_all(sent, 'bulk', split_axis=0, concat_axis=0, tiled=True)  14.4 us
    pallas_call x1, Pallas kernels, return_nodes(): pl.pallas_call(functools.partial(return_kernel, owners, windows, given_pa...  14.2 us
    unnamed x10, local copies, waits for them, and re-layouts  7.44 us

profile of v1, /device:TPU:0, one launch (start us, length us, event | category | flops | bytes accessed | tf_op | source)
XLA Modules:
  0.0 97.4 jit_solution(3777441363357799485)
XLA Ops:
  0.0 0.0 copy-start.1
  0.0 0.9 copy-done.1
  1.0 0.0 copy-start.2
  1.0 0.9 copy-done.2
  1.9 0.0 copy-start.3
  1.9 0.8 copy-done.3
  2.7 0.0 copy-start.4
  2.7 0.8 copy-done.4
  3.5 14.4 %route.1 = (f32[8,120,128]{2,1,0:T(8,128)S(1)}, s32[128,128]{1,0:T(8,128)S(1)}, s32[8,128]{1,0:T(8,128)S(1)}) custom-call(s32[128,128]{1,0:T(8,128)S(1)} %bitcast.8, s32[128,128]{1,0:T(8,128)S(1)} %bitcast.9, s32[2,16384]{1,0:T(2,128)S(1)} %copy-done.2, f32[3,16384]{1,0:T(4,128)S(1)} %copy-done.1), custom_call_target="tpu_custom_call" | custom-call | tf_op jit(solution)/shard_map/route/pallas_call | solution.py:107
  17.9 14.4 %all_to_all.10 = f32[8,120,128]{2,1,0:T(8,128)S(1)} all-to-all(f32[8,120,128]{2,1,0:T(8,128)S(1)} %get-tuple-element.10), channel_id=1, replica_groups=mesh['dom'=4,'bulk'=8] {'bulk'}, dimensions={0} | all-to-all | bytes 983040 | tf_op jit(solution)/shard_map/all_to_all | solution.py:308
  32.3 0.0 copy-start
  32.3 3.9 %copy-done = f32[2500,1024]{1,0:T(8,128)S(1)} copy-done((f32[2500,1024]{1,0:T(8,128)S(1)}, f32[2500,1024]{1,0:T(8,128)}, u32[]{:S(2)}) %copy-start) | copy-done | bytes 10240024
  36.2 32.4 %project.1 = f32[1472,128]{1,0:T(8,128)S(1)} custom-call(f32[960,128]{1,0:T(8,128)S(1)} %bitcast.7, f32[2500,1024]{1,0:T(8,128)S(1)} %copy-done), custom_call_target="tpu_custom_call" | custom-call | tf_op jit(solution)/shard_map/project/pallas_call | solution.py:235
  68.6 14.6 %all_to_all.11 = f32[8,184,128]{2,1,0:T(8,128)S(1)} all-to-all(f32[8,184,128]{2,1,0:T(8,128)S(1)} %bitcast.6), channel_id=1, replica_groups=mesh['dom'=4,'bulk'=8] {'bulk'}, dimensions={0} | all-to-all | bytes 1507328 | tf_op jit(solution)/shard_map/all_to_all | solution.py:310
  83.2 14.2 %give_back.1 = f32[9,16384]{1,0:T(8,128)} custom-call(s32[128,128]{1,0:T(8,128)S(1)} %get-tuple-element.8.key_ref, s32[8,128]{1,0:T(8,128)S(1)} %get-tuple-element.9.first_smem, f32[1472,128]{1,0:T(8,128)S(1)} %bitcast.5), custom_call_target="tpu_custom_call" | custom-call | tf_op jit(solution)/shard_map/give_back/pallas_call | solution.py:286
Async XLA Ops:
  0.0 0.9 copy-start.1
  1.0 0.9 copy-start.2
  1.9 0.8 copy-start.3
  2.7 0.8 copy-start.4
  32.3 3.9 %copy-start = (f32[2500,1024]{1,0:T(8,128)S(1)}, f32[2500,1024]{1,0:T(8,128)}, u32[]{:S(2)}) copy-start(f32[2500,1024]{1,0:T(8,128)} %net_ref.1) | copy-start | bytes 30720004

commit v2 on v1

v2 whole, which is shorter than its diff:
```python
import functools

import jax
import jax.numpy as jnp
from jax import lax
from jax.experimental import pallas as pl
from jax.experimental.pallas import tpu as pltpu
from jax.sharding import PartitionSpec as P

SPANS = 16
LEVELS = 16
ITERS = 4
LANES = 128
SENT = 6
GIVEN = 9
UNROLL = 8

damping = 0.1


def round_up(value, unit):
    return -(-value // unit) * unit


def iota(shape, dim):
    return lax.broadcasted_iota(jnp.int32, shape, dim)


def take_lanes(rows, lane):
    return jnp.take_along_axis(rows, lane, axis=1, mode="promise_in_bounds")


def route_kernel(owners, windows, patch_dev, patch_hbm, span_hbm, grid_hbm, target_hbm, net_hbm,
                 sent_ref, key_ref, first_ref, net_ref,
                 patch_ref, span_ref, grid_ref, target_ref,
                 code_ref, load_ref, slot_ref, first_smem, in_sem, net_sem, first_sem):
    copies = []
    for k, (source, to) in enumerate(
            ((patch_hbm, patch_ref), (span_hbm, span_ref), (grid_hbm, grid_ref), (target_hbm, target_ref))):
        copies.append(pltpu.make_async_copy(source, to, in_sem.at[k]))
        copies[-1].start()
    chunks = net_hbm.shape[1] // LANES
    patch_pad = net_ref.shape[0] // chunks
    loads = []
    for c in range(chunks):
        loads.append(pltpu.make_async_copy(
            net_hbm.at[:, pl.ds(c * LANES, LANES)], net_ref.at[pl.ds(c * patch_pad, patch_dev), :], net_sem.at[c]))
        loads[-1].start()
    slot_ref[...] = jnp.zeros_like(slot_ref)
    blocks = patch_ref.shape[0]
    copies[0].wait()
    patch = patch_ref[...]
    owner = jnp.zeros_like(patch)
    for o in range(1, owners):
        owner += (patch >= o * patch_dev).astype(jnp.int32)

    lane = iota((LANES, LANES), 1)
    sub = iota((LANES, LANES), 0)
    upto = (sub <= lane).astype(jnp.bfloat16)
    every = jnp.ones((LANES, LANES), jnp.bfloat16)
    counter = jnp.concatenate([upto, every], axis=1)
    earlier = (iota((blocks, blocks), 1) < iota((blocks, blocks), 0)).astype(jnp.bfloat16)
    blane = iota((blocks, LANES), 1)
    diagonal = iota((blocks, blocks), 0) == iota((blocks, blocks), 1)

    key = jnp.zeros_like(patch)
    for o in range(owners):
        mine = owner == o
        mask = mine.astype(jnp.bfloat16)
        counts = jnp.dot(mask, counter, preferred_element_type=jnp.float32)
        total = counts[:, LANES:]
        offset = jnp.dot(earlier, total.astype(jnp.bfloat16), preferred_element_type=jnp.float32).astype(jnp.int32)
        before = counts[:, :LANES].astype(jnp.int32) - mine.astype(jnp.int32)
        total = total.astype(jnp.int32)
        edge = offset & (LANES - 1)
        key = jnp.where(mine, before + edge + 2 * LANES * o, key)
        first = jnp.sum(jnp.where(diagonal, offset.astype(jnp.float32), 0.0), axis=0, keepdims=True)
        first_ref[o:o + 1, :] = first.astype(jnp.int32) >> 7
        word = jnp.where(mine, blane + LANES * (blane - before), 0)
        for bit in range(7):
            moves = 1 << (7 + bit)
            coming = pltpu.roll(word, LANES - (1 << bit), 1)
            word = jnp.where((coming & moves) != 0, coming, jnp.where((word & moves) != 0, 0, word))
        rank = (blane - edge) & (LANES - 1)
        source = take_lanes(word & (LANES - 1), rank)
        valid = rank < total
        code_ref[o * blocks:(o + 1) * blocks, :] = source + jnp.where(valid, jnp.where(blane >= edge, 128, 256), 0)

    key_ref[...] = key
    copy = pltpu.make_async_copy(first_ref, first_smem, first_sem)
    copy.start()
    for waiting in copies[1:]:
        waiting.wait()
    span = span_ref[...]
    row = (2 * ((span >> 1) * patch_pad + patch - owner * patch_dev) + (span & 1)).astype(jnp.float32)
    for b in range(blocks):
        load_ref[8 * b:8 * b + 3, :] = target_ref[:, b * LANES:(b + 1) * LANES]
        load_ref[8 * b + 3:8 * b + 5, :] = (grid_ref[:, b * LANES:(b + 1) * LANES].astype(jnp.float32) + 0.5) * (1.0 / LEVELS)
        load_ref[8 * b + 5:8 * b + 6, :] = row[b:b + 1, :]
    copy.wait()

    def place(step, carry):
        for k in range(UNROLL):
            b = step * UNROLL + k
            load = load_ref[pl.ds(pl.multiple_of(8 * b, 8), 8), :]
            for o in range(owners):
                code = jnp.broadcast_to(code_ref[pl.ds(o * blocks + b, 1), :], (8, LANES))
                moved = take_lanes(load, code & (LANES - 1))
                base = pl.multiple_of((o * (windows + 1) + first_smem[o, b]) * 8, 8)
                pltpu.store(slot_ref.at[pl.ds(base, 8), :], moved, mask=(code & 128) != 0)
                pltpu.store(slot_ref.at[pl.ds(base + 8, 8), :], moved, mask=(code & 256) != 0)
        return carry

    lax.fori_loop(0, blocks // UNROLL, place, 0)

    for o in range(owners):
        for c in range(SENT):
            for w in range(0, windows, 8):
                size = min(8, windows - w)
                rows = slot_ref[pl.ds((o * (windows + 1) + w) * 8 + c, size, stride=8), :]
                sent_ref[o, c * windows + w:c * windows + w + size, :] = rows
    for waiting in loads:
        waiting.wait()


def route(node_patch, node_span, start_grid, target, net, owners, windows):
    nodes = node_patch.shape[0]
    blocks = nodes // LANES
    patch_dev = net.shape[0]
    chunks = net.shape[1] // LANES
    patch_pad = round_up(patch_dev, 8)
    return pl.pallas_call(
        functools.partial(route_kernel, owners, windows, patch_dev),
        out_shape=(
            jax.ShapeDtypeStruct((owners, SENT * windows, LANES), jnp.float32),
            jax.ShapeDtypeStruct((blocks, LANES), jnp.int32),
            jax.ShapeDtypeStruct((owners, blocks), jnp.int32),
            jax.ShapeDtypeStruct((chunks * patch_pad, LANES), jnp.float32),
        ),
        in_specs=[pl.BlockSpec(memory_space=pltpu.HBM)] * 5,
        out_specs=[pl.BlockSpec(memory_space=pltpu.VMEM)] * 4,
        scratch_shapes=[
            pltpu.VMEM((blocks, LANES), jnp.int32),
            pltpu.VMEM((blocks, LANES), jnp.int32),
            pltpu.VMEM(start_grid.shape, jnp.int32),
            pltpu.VMEM(target.shape, jnp.float32),
            pltpu.VMEM((owners * blocks, LANES), jnp.int32),
            pltpu.VMEM((8 * blocks, LANES), jnp.float32),
            pltpu.VMEM((owners * (windows + 1) * 8, LANES), jnp.float32),
            pltpu.SMEM((owners, blocks), jnp.int32),
            pltpu.SemaphoreType.DMA((4,)),
            pltpu.SemaphoreType.DMA((chunks,)),
            pltpu.SemaphoreType.DMA,
        ],
        compiler_params=pltpu.CompilerParams(vmem_limit_bytes=40 * 2**20),
        name="route",
    )(node_patch.reshape(blocks, LANES), node_span.reshape(blocks, LANES), start_grid, target, net)


def bernstein(param):
    other = 1.0 - param
    square, cross, low = other * other, param * other, param * param
    value = (other * square, 3.0 * cross * other, 3.0 * param * cross, param * low)
    slope = (-3.0 * square, 3.0 * square - 6.0 * cross, 6.0 * cross - 3.0 * low, 3.0 * low)
    return value, slope


def weighted(weights, values):
    return (weights[0] * values[0] + weights[1] * values[1]) + (weights[2] * values[2] + weights[3] * values[3])


def surface(read, upar, vpar, answer):
    base_u, slope_u = bernstein(upar)
    base_v, slope_v = bernstein(vpar)
    yield
    point, along_u, along_v = [], [], []
    for c in range(4):
        mixed, mixed_u = [], []
        for j in range(4):
            column = [read(c * 16 + i * 4 + j) for i in range(4)]
            mixed.append(weighted(base_u, column))
            mixed_u.append(weighted(slope_u, column))
            yield
        point.append(weighted(base_v, mixed))
        along_u.append(weighted(base_v, mixed_u))
        along_v.append(weighted(slope_v, mixed))
        yield
    inverse = 1.0 / point[3]
    position = [point[c] * inverse for c in range(3)]
    yield
    tangent_u = [(along_u[c] - position[c] * along_u[3]) * inverse for c in range(3)]
    tangent_v = [(along_v[c] - position[c] * along_v[3]) * inverse for c in range(3)]
    yield
    answer.extend((position, tangent_u, tangent_v))


def inner(left, right):
    return left[0] * right[0] + left[1] * right[1] + left[2] * right[2]


def project(read, goal, start, finish):
    upar, vpar = start()
    goal = goal()
    for _ in range(ITERS):
        answer = []
        yield from surface(read, upar, vpar, answer)
        position, tangent_u, tangent_v = answer
        miss = [position[c] - goal[c] for c in range(3)]
        grad_u = inner(tangent_u, miss)
        grad_v = inner(tangent_v, miss)
        yield
        h_uu = inner(tangent_u, tangent_u) + damping
        h_vv = inner(tangent_v, tangent_v) + damping
        h_uv = inner(tangent_u, tangent_v)
        yield
        inverse = 1.0 / (h_uu * h_vv - h_uv * h_uv)
        upar = jnp.clip(upar - (h_vv * grad_u - h_uv * grad_v) * inverse, 0.0, 1.0)
        vpar = jnp.clip(vpar - (h_uu * grad_v - h_uv * grad_u) * inverse, 0.0, 1.0)
        yield
    answer = []
    yield from surface(read, upar, vpar, answer)
    finish(answer[0] + answer[1] + answer[2])


PROJECT_STEPS = ITERS * 27 + 25


def project_kernel(sources, windows, given_pad, got_ref, net_ref, out_ref,
                   index_ref, index_even, index_odd, tile_ref, coeff_even, coeff_odd, index_sem):
    groups = sources // 8
    sent = SENT * windows
    total = windows * groups
    indices, coeffs = (index_even, index_odd), (coeff_even, coeff_odd)

    def arrived(t, c):
        w, g = t // groups, t % groups
        return got_ref[pl.ds(g * 8 * sent + c * windows + w, 8, stride=sent), :]

    def fetch(t, parity):
        return pltpu.make_async_copy(
            index_ref.at[pl.ds(pl.multiple_of(8 * t, 8), 8), :], indices[parity], index_sem.at[parity])

    def gather(t, parity):
        index, coeff = indices[parity], coeffs[parity]
        odd = (arrived(t, 5).astype(jnp.int32) & 1) == 1
        for s in range(8):
            for i in range(LANES):
                tile_ref[s * LANES + i:s * LANES + i + 1, :] = net_ref[pl.ds(index[s, i], 1), :]
                yield
            both = tile_ref[s * LANES:(s + 1) * LANES, :].T
            coeff[pl.ds(s, 64, stride=8), :] = jnp.where(odd[s:s + 1, :], both[64:, :], both[:64, :])

    def solve(t, parity):
        def finish(result):
            w, g = t // groups, t % groups
            for c in range(GIVEN):
                at = (c + 1) % GIVEN
                out_ref[pl.ds(g * 8 * given_pad + at * windows + w, 8, stride=given_pad), :] = result[c]

        return project(
            lambda k: coeffs[parity][8 * k:8 * k + 8, :],
            lambda: [arrived(t, c) for c in range(3)],
            lambda: (arrived(t, 3), arrived(t, 4)),
            finish)

    def interleave(rows, steps):
        done = 0
        for k, _ in enumerate(rows):
            while done < PROJECT_STEPS and done * 8 * LANES <= k * PROJECT_STEPS:
                next(steps, None)
                done += 1
        for _ in steps:
            pass

    for t in range(total):
        index_ref[8 * t:8 * t + 8, :] = arrived(t, 5).astype(jnp.int32) >> 1
    fetch(0, 0).start()
    fetch(1, 1).start()
    fetch(0, 0).wait()
    for _ in gather(0, 0):
        pass

    def pair(i, carry):
        t = 2 * i
        fetch(t + 1, 1).wait()
        fetch(t + 2, 0).start()
        interleave(gather(t + 1, 1), solve(t, 0))
        fetch(t + 2, 0).wait()
        fetch(t + 3, 1).start()
        interleave(gather(t + 2, 0), solve(t + 1, 1))
        return carry

    lax.fori_loop(0, total // 2 - 1, pair, 0)
    fetch(total - 1, 1).wait()
    interleave(gather(total - 1, 1), solve(total - 2, 0))
    for _ in solve(total - 1, 1):
        pass


def project_nodes(got, net, windows, given_pad):
    sources = got.shape[0]
    tiles = windows * sources
    return pl.pallas_call(
        functools.partial(project_kernel, sources, windows, given_pad),
        out_shape=jax.ShapeDtypeStruct((sources * given_pad, LANES), jnp.float32),
        in_specs=[pl.BlockSpec(memory_space=pltpu.VMEM)] * 2,
        out_specs=pl.BlockSpec(memory_space=pltpu.VMEM),
        scratch_shapes=[
            pltpu.VMEM((tiles, LANES), jnp.int32),
            pltpu.SMEM((8, LANES), jnp.int32),
            pltpu.SMEM((8, LANES), jnp.int32),
            pltpu.VMEM((8 * LANES, LANES), jnp.float32),
            pltpu.VMEM((64 * 8, LANES), jnp.float32),
            pltpu.VMEM((64 * 8, LANES), jnp.float32),
            pltpu.SemaphoreType.DMA((2,)),
        ],
        compiler_params=pltpu.CompilerParams(vmem_limit_bytes=30 * 2**20),
        name="project",
    )(got.reshape(sources * SENT * windows, LANES), net)


def return_kernel(owners, windows, given_pad, key_ref, first_smem, got_ref, out_ref):
    blocks = key_ref.shape[0]
    sub = iota((8, LANES), 0)

    def fetch(step, carry):
        for k in range(UNROLL):
            b = step * UNROLL + k
            key = jnp.broadcast_to(key_ref[pl.ds(b, 1), :], (8, LANES))
            lane = key & (LANES - 1)
            key = key >> 7
            rest = jnp.where(sub < 2, key - sub, -1)
            main = jnp.zeros((8, LANES), jnp.float32)
            last = jnp.zeros((8, LANES), jnp.float32)
            for o in range(owners):
                base = o * given_pad + first_smem[o, b]
                moved = take_lanes(got_ref[pl.ds(base, 8), :], lane)
                last = jnp.where(rest == 2 * o, moved, last)
                for step_over in range(2):
                    rows = got_ref[pl.ds(base + windows + step_over, 8, stride=windows), :]
                    main = jnp.where(key == 2 * o + step_over, take_lanes(rows, lane), main)
            at = pl.ds(pl.multiple_of(b * LANES, LANES), LANES)
            out_ref[0:8, at] = main
            out_ref[8:9, at] = jnp.sum(last, axis=0, keepdims=True)
        return carry

    lax.fori_loop(0, blocks // UNROLL, fetch, 0)


def return_nodes(key, first, got, windows, given_pad):
    owners, blocks = first.shape
    return pl.pallas_call(
        functools.partial(return_kernel, owners, windows, given_pad),
        out_shape=jax.ShapeDtypeStruct((GIVEN, blocks * LANES), jnp.float32),
        in_specs=[
            pl.BlockSpec(memory_space=pltpu.VMEM),
            pl.BlockSpec(memory_space=pltpu.SMEM),
            pl.BlockSpec(memory_space=pltpu.VMEM),
        ],
        out_specs=pl.BlockSpec(memory_space=pltpu.VMEM),
        compiler_params=pltpu.CompilerParams(vmem_limit_bytes=40 * 2**20),
        name="give_back",
    )(key, first, got.reshape(owners * given_pad, LANES))


def body(node_patch, node_span, start_grid, target, net):
    owners = lax.axis_size("bulk")
    windows = node_patch.shape[0] * 5 // 32 // LANES
    given_pad = round_up(GIVEN * windows + 1, 8)
    sent, key, first, net_rows = route(node_patch, node_span, start_grid, target, net, owners, windows)
    got = lax.all_to_all(sent, "bulk", split_axis=0, concat_axis=0, tiled=True)
    placed = project_nodes(got, net_rows, windows, given_pad)
    answered = lax.all_to_all(
        placed.reshape(owners, given_pad, LANES), "bulk", split_axis=0, concat_axis=0, tiled=True)
    return return_nodes(key, first, answered, windows, given_pad)


def solution(mesh):
    return jax.shard_map(
        body,
        mesh=mesh,
        in_specs=(
            P(("dom", "bulk")),
            P(("dom", "bulk")),
            P(None, ("dom", "bulk")),
            P(None, ("dom", "bulk")),
            P("bulk", None),
        ),
        out_specs=P(None, ("dom", "bulk")),
        check_vma=False,
    )
```

time: 97.8 us -> 75.4 us (0.77)
  Pallas kernels: 61 us -> 42.5 us
  local copies, waits for them, and re-layouts: 7.44 us -> 3.53 us
    pallas_call x1, Pallas kernels: 14.2 us -> 6.33 us  [return_nodes(): pl.pallas_call(functools.partial(return_kernel, owners, windows, given_pa...]
    pallas_call x1, Pallas kernels: 14.4 us -> 7.04 us  [route(): pl.pallas_call(functools.partial(route_kernel, owners, windows, patch_dev...]
    unnamed x10 -> x8, local copies, waits for them, and re-layouts: 7.44 us -> 3.53 us
    pallas_call x1, Pallas kernels: 32.4 us -> 29.2 us  [project_nodes(): pl.pallas_call(functools.partial(project_kernel, sources, windows, given_...]
where the time goes in v2:
time: 75.4 us; the launch traced here: 75.1 us
  Pallas kernels  42.5 us (56%)
  blocking collectives  29 us (38%)
  local copies, waits for them, and re-layouts  3.53 us (5%)
    pallas_call x1, Pallas kernels, project_nodes(): pl.pallas_call(functools.partial(project_kernel, sources, windows, given_...  29.2 us
    all_to_all x1, blocking collectives, body(): lax.all_to_all(placed.reshape(owners, given_pad, LANES), 'bulk', split_ax...  14.6 us
    all_to_all x1, blocking collectives, body(): got = lax.all_to_all(sent, 'bulk', split_axis=0, concat_axis=0, tiled=True)  14.4 us
    pallas_call x1, Pallas kernels, route(): pl.pallas_call(functools.partial(route_kernel, owners, windows, patch_dev...  7.04 us
    pallas_call x1, Pallas kernels, return_nodes(): pl.pallas_call(functools.partial(return_kernel, owners, windows, given_pa...  6.33 us
    unnamed x8, local copies, waits for them, and re-layouts  3.53 us

profile of v2, /device:TPU:0, one launch (start us, length us, event | category | flops | bytes accessed | tf_op | source)
XLA Modules:
  0.0 75.1 jit_solution(5089735098535708585)
XLA Ops:
  0.0 0.0 copy-start
  0.0 0.9 %copy-done = f32[3,16384]{1,0:T(4,128)S(1)} copy-done((f32[3,16384]{1,0:T(4,128)S(1)}, f32[3,16384]{1,0:T(4,128)}, u32[]{:S(2)}) %copy-start) | copy-done | bytes 196632
  1.0 0.0 copy-start.1
  1.0 0.9 %copy-done.1 = s32[2,16384]{1,0:T(2,128)S(1)} copy-done((s32[2,16384]{1,0:T(2,128)S(1)}, s32[2,16384]{1,0:T(2,128)}, u32[]{:S(2)}) %copy-start.1) | copy-done | bytes 131096
  1.9 0.0 copy-start.2
  1.9 0.8 %copy-done.2 = s32[16384]{0:T(1024)S(1)} copy-done((s32[16384]{0:T(1024)S(1)}, s32[16384]{0:T(1024)}, u32[]{:S(2)}) %copy-start.2) | copy-done | bytes 65560
  2.7 0.0 copy-start.3
  2.7 0.8 %copy-done.3 = s32[16384]{0:T(1024)S(1)} copy-done((s32[16384]{0:T(1024)S(1)}, s32[16384]{0:T(1024)}, u32[]{:S(2)}) %copy-start.3) | copy-done | bytes 65560
  3.5 7.0 %route.1 = (f32[8,120,128]{2,1,0:T(8,128)S(1)}, s32[128,128]{1,0:T(8,128)S(1)}, s32[8,128]{1,0:T(8,128)S(1)}, f32[20032,128]{1,0:T(8,128)S(1)}) custom-call(s32[128,128]{1,0:T(8,128)S(1)} %bitcast.8, s32[128,128]{1,0:T(8,128)S(1)} %bitcast.9, s32[2,16384]{1,0:T(2,128)S(1)} %copy-done.1, f32[3,16384]{1,0:T(4,128)S(1)} %copy-done, f32[2500,1024]{1,0:T(8,128)} %net_hbm.1), custom_call_target="tpu_custom_call" | custom-call | tf_op jit(solution)/shard_map/route/pallas_call | solution.py:132
  10.6 14.4 %all_to_all.10 = f32[8,120,128]{2,1,0:T(8,128)S(1)} all-to-all(f32[8,120,128]{2,1,0:T(8,128)S(1)} %get-tuple-element.11), channel_id=1, replica_groups=mesh['dom'=4,'bulk'=8] {'bulk'}, dimensions={0} | all-to-all | bytes 983040 | tf_op jit(solution)/shard_map/all_to_all | solution.py:371
  24.9 29.2 %project.1 = f32[1472,128]{1,0:T(8,128)S(1)} custom-call(f32[960,128]{1,0:T(8,128)S(1)} %bitcast.7, f32[20032,128]{1,0:T(8,128)S(1)} %get-tuple-element.12.net_ref), custom_call_target="tpu_custom_call" | custom-call | tf_op jit(solution)/shard_map/project/pallas_call | solution.py:303
  54.1 14.6 %all_to_all.11 = f32[8,184,128]{2,1,0:T(8,128)S(1)} all-to-all(f32[8,184,128]{2,1,0:T(8,128)S(1)} %bitcast.6), channel_id=1, replica_groups=mesh['dom'=4,'bulk'=8] {'bulk'}, dimensions={0} | all-to-all | bytes 1507328 | tf_op jit(solution)/shard_map/all_to_all | solution.py:373
  68.7 6.3 %give_back.1 = f32[9,16384]{1,0:T(8,128)} custom-call(s32[128,128]{1,0:T(8,128)S(1)} %get-tuple-element.9.key_ref, s32[8,128]{1,0:T(8,128)S(1)} %get-tuple-element.10.first_smem, f32[1472,128]{1,0:T(8,128)S(1)} %bitcast.5), custom_call_target="tpu_custom_call" | custom-call | tf_op jit(solution)/shard_map/give_back/pallas_call | solution.py:352
Async XLA Ops:
  0.0 0.9 %copy-start = (f32[3,16384]{1,0:T(4,128)S(1)}, f32[3,16384]{1,0:T(4,128)}, u32[]{:S(2)}) copy-start(f32[3,16384]{1,0:T(4,128)} %target_hbm.1) | copy-start | bytes 589828
  1.0 0.9 %copy-start.1 = (s32[2,16384]{1,0:T(2,128)S(1)}, s32[2,16384]{1,0:T(2,128)}, u32[]{:S(2)}) copy-start(s32[2,16384]{1,0:T(2,128)} %grid_hbm.1) | copy-start | bytes 393220
  1.9 0.8 %copy-start.2 = (s32[16384]{0:T(1024)S(1)}, s32[16384]{0:T(1024)}, u32[]{:S(2)}) copy-start(s32[16384]{0:T(1024)} %param.5) | copy-start | bytes 196612
  2.7 0.8 %copy-start.3 = (s32[16384]{0:T(1024)S(1)}, s32[16384]{0:T(1024)}, u32[]{:S(2)}) copy-start(s32[16384]{0:T(1024)} %param.6) | copy-start | bytes 196612

commit v3 on v2

--- a/solution.py
+++ b/solution.py
@@ -13,7 +13,7 @@
 LANES = 128
 SENT = 6
 GIVEN = 9
-UNROLL = 8
+UNROLL = 16
 
 damping = 0.1
 
@@ -152,9 +152,10 @@
             pltpu.SemaphoreType.DMA((chunks,)),
             pltpu.SemaphoreType.DMA,
         ],
-        compiler_params=pltpu.CompilerParams(vmem_limit_bytes=40 * 2**20),
+        compiler_params=pltpu.CompilerParams(vmem_limit_bytes=16 * 2**20),
         name="route",
-    )(node_patch.reshape(blocks, LANES), node_span.reshape(blocks, LANES), start_grid, target, net)
+    )(*(pltpu.with_memory_space_constraint(x, pltpu.HBM) for x in (
+        node_patch.reshape(blocks, LANES), node_span.reshape(blocks, LANES), start_grid, target, net)))
 
 
 def bernstein(param):
@@ -226,31 +227,38 @@
 
 
 def project_kernel(sources, windows, given_pad, got_ref, net_ref, out_ref,
-                   index_ref, index_even, index_odd, tile_ref, coeff_even, coeff_odd, index_sem):
+                   index_ref, index_0, index_1, index_2, index_3, tile_even, tile_odd, coeff_even, coeff_odd, index_sem):
     groups = sources // 8
     sent = SENT * windows
     total = windows * groups
-    indices, coeffs = (index_even, index_odd), (coeff_even, coeff_odd)
+    indices = (index_0, index_1, index_2, index_3)
+    tiles, coeffs = (tile_even, tile_odd), (coeff_even, coeff_odd)
+    depth = len(indices)
 
     def arrived(t, c):
         w, g = t // groups, t % groups
         return got_ref[pl.ds(g * 8 * sent + c * windows + w, 8, stride=sent), :]
 
-    def fetch(t, parity):
+    def fetch(t, k):
         return pltpu.make_async_copy(
-            index_ref.at[pl.ds(pl.multiple_of(8 * t, 8), 8), :], indices[parity], index_sem.at[parity])
-
-    def gather(t, parity):
-        index, coeff = indices[parity], coeffs[parity]
+            index_ref.at[pl.ds(pl.multiple_of(8 * t, 8), 8), :], indices[k % depth], index_sem.at[k % depth])
+
+    def gather(k):
+        index, tile = indices[k % depth], tiles[k % 2]
+        for s in range(8):
+            for i in range(LANES):
+                tile[s * LANES + i:s * LANES + i + 1, :] = net_ref[pl.ds(index[s, i], 1), :]
+                yield
+
+    def turn(t, k):
+        tile, coeff = tiles[k % 2], coeffs[k % 2]
         odd = (arrived(t, 5).astype(jnp.int32) & 1) == 1
         for s in range(8):
-            for i in range(LANES):
-                tile_ref[s * LANES + i:s * LANES + i + 1, :] = net_ref[pl.ds(index[s, i], 1), :]
-                yield
-            both = tile_ref[s * LANES:(s + 1) * LANES, :].T
+            both = tile[s * LANES:(s + 1) * LANES, :].T
             coeff[pl.ds(s, 64, stride=8), :] = jnp.where(odd[s:s + 1, :], both[64:, :], both[:64, :])
-
-    def solve(t, parity):
+            yield
+
+    def solve(t, k):
         def finish(result):
             w, g = t // groups, t % groups
             for c in range(GIVEN):
@@ -258,43 +266,57 @@
                 out_ref[pl.ds(g * 8 * given_pad + at * windows + w, 8, stride=given_pad), :] = result[c]
 
         return project(
-            lambda k: coeffs[parity][8 * k:8 * k + 8, :],
+            lambda e: coeffs[k % 2][8 * e:8 * e + 8, :],
             lambda: [arrived(t, c) for c in range(3)],
             lambda: (arrived(t, 3), arrived(t, 4)),
             finish)
 
-    def interleave(rows, steps):
-        done = 0
-        for k, _ in enumerate(rows):
-            while done < PROJECT_STEPS and done * 8 * LANES <= k * PROJECT_STEPS:
-                next(steps, None)
-                done += 1
-        for _ in steps:
-            pass
+    def interleave(*works):
+        order = sorted(((at + 0.5) / size, k) for k, (_, size) in enumerate(works) for at in range(size))
+        for _, k in order:
+            next(works[k][0], None)
+        for work, _ in works:
+            for _ in work:
+                pass
+
+    def gathering(k):
+        return gather(k), 8 * LANES
+
+    def turning(t, k):
+        return turn(t, k), 8
+
+    def solving(t, k):
+        return solve(t, k), PROJECT_STEPS
 
     for t in range(total):
         index_ref[8 * t:8 * t + 8, :] = arrived(t, 5).astype(jnp.int32) >> 1
-    fetch(0, 0).start()
-    fetch(1, 1).start()
+        if t < depth:
+            fetch(t, t).start()
+    index_ref[8 * total:8 * total + 8, :] = jnp.zeros((8, LANES), jnp.int32)
     fetch(0, 0).wait()
-    for _ in gather(0, 0):
-        pass
-
-    def pair(i, carry):
-        t = 2 * i
-        fetch(t + 1, 1).wait()
-        fetch(t + 2, 0).start()
-        interleave(gather(t + 1, 1), solve(t, 0))
-        fetch(t + 2, 0).wait()
-        fetch(t + 3, 1).start()
-        interleave(gather(t + 2, 0), solve(t + 1, 1))
+    interleave(gathering(0))
+    fetch(1, 1).wait()
+    fetch(depth, depth).start()
+    interleave(gathering(1), turning(0, 0))
+
+    def steps(i, carry):
+        for k in range(depth):
+            t = depth * i + k
+            fetch(t + 2, k + 2).wait()
+            fetch(t + depth + 1, k + 1).start()
+            interleave(gathering(k + 2), turning(t + 1, k + 1), solving(t, k))
         return carry
 
-    lax.fori_loop(0, total // 2 - 1, pair, 0)
-    fetch(total - 1, 1).wait()
-    interleave(gather(total - 1, 1), solve(total - 2, 0))
-    for _ in solve(total - 1, 1):
-        pass
+    lax.fori_loop(0, total // depth - 1, steps, 0)
+    for t in range(total - depth, total):
+        if t + 2 < total:
+            fetch(t + 2, t + 2).wait()
+            interleave(gathering(t + 2), turning(t + 1, t + 1), solving(t, t))
+        elif t + 1 < total:
+            interleave(turning(t + 1, t + 1), solving(t, t))
+        else:
+            interleave(solving(t, t))
+    fetch(total, total).wait()
 
 
 def project_nodes(got, net, windows, given_pad):
@@ -306,15 +328,18 @@
         in_specs=[pl.BlockSpec(memory_space=pltpu.VMEM)] * 2,
         out_specs=pl.BlockSpec(memory_space=pltpu.VMEM),
         scratch_shapes=[
-            pltpu.VMEM((tiles, LANES), jnp.int32),
+            pltpu.VMEM((tiles + 8, LANES), jnp.int32),
+            pltpu.SMEM((8, LANES), jnp.int32),
+            pltpu.SMEM((8, LANES), jnp.int32),
             pltpu.SMEM((8, LANES), jnp.int32),
             pltpu.SMEM((8, LANES), jnp.int32),
             pltpu.VMEM((8 * LANES, LANES), jnp.float32),
+            pltpu.VMEM((8 * LANES, LANES), jnp.float32),
             pltpu.VMEM((64 * 8, LANES), jnp.float32),
             pltpu.VMEM((64 * 8, LANES), jnp.float32),
-            pltpu.SemaphoreType.DMA((2,)),
+            pltpu.SemaphoreType.DMA((4,)),
         ],
-        compiler_params=pltpu.CompilerParams(vmem_limit_bytes=30 * 2**20),
+        compiler_params=pltpu.CompilerParams(vmem_limit_bytes=24 * 2**20),
         name="project",
     )(got.reshape(sources * SENT * windows, LANES), net)
 
@@ -358,7 +383,7 @@
             pl.BlockSpec(memory_space=pltpu.VMEM),
         ],
         out_specs=pl.BlockSpec(memory_space=pltpu.VMEM),
-        compiler_params=pltpu.CompilerParams(vmem_limit_bytes=40 * 2**20),
+        compiler_params=pltpu.CompilerParams(vmem_limit_bytes=16 * 2**20),
         name="give_back",
     )(key, first, got.reshape(owners * given_pad, LANES))
 

time: 75.4 us -> 61.1 us (0.81)
  Pallas kernels: 42.5 us -> 31.9 us
  local copies, waits for them, and re-layouts: 3.53 us -> 0 us
    pallas_call x1, Pallas kernels: 29.2 us -> 16.7 us  [project_nodes(): pl.pallas_call(functools.partial(project_kernel, sources, windows, given_...]
    unnamed x8 -> x0, local copies, waits for them, and re-layouts: 3.53 us -> none
    pallas_call x1, Pallas kernels: 7.04 us -> 9.43 us  [route(): pl.pallas_call(functools.partial(route_kernel, owners, windows, patch_dev...]
where the time goes in v3:
time: 61.1 us; the launch traced here: 60.9 us
  Pallas kernels  31.9 us (52%)
  blocking collectives  29 us (47%)
    pallas_call x1, Pallas kernels, project_nodes(): pl.pallas_call(functools.partial(project_kernel, sources, windows, given_...  16.7 us
    all_to_all x1, blocking collectives, body(): lax.all_to_all(placed.reshape(owners, given_pad, LANES), 'bulk', split_ax...  14.6 us
    all_to_all x1, blocking collectives, body(): got = lax.all_to_all(sent, 'bulk', split_axis=0, concat_axis=0, tiled=True)  14.4 us
    pallas_call x1, Pallas kernels, route(): pl.pallas_call(functools.partial(route_kernel, owners, windows, patch_dev...  9.43 us
    pallas_call x1, Pallas kernels, return_nodes(): pl.pallas_call(functools.partial(return_kernel, owners, windows, given_pa...  5.78 us

profile of v3, /device:TPU:0, one launch (start us, length us, event | category | flops | bytes accessed | tf_op | source)
XLA Modules:
  0.0 60.9 jit_solution(6000522311519973172)
XLA Ops:
  0.0 9.4 %route.1 = (f32[8,120,128]{2,1,0:T(8,128)S(1)}, s32[128,128]{1,0:T(8,128)S(1)}, s32[8,128]{1,0:T(8,128)S(1)}, f32[20032,128]{1,0:T(8,128)S(1)}) custom-call(s32[128,128]{1,0:T(8,128)} %bitcast.8, s32[128,128]{1,0:T(8,128)} %bitcast.9, s32[2,16384]{1,0:T(2,128)} %grid_hbm.1, f32[3,16384]{1,0:T(4,128)} %target_hbm.1, f32[2500,1024]{1,0:T(8,128)} %net_hbm.1), custom_call_target="tpu_custom_call" | custom-call | tf_op jit(solution)/shard_map/route/pallas_call | solution.py:132
  9.4 14.4 %all_to_all.10 = f32[8,120,128]{2,1,0:T(8,128)S(1)} all-to-all(f32[8,120,128]{2,1,0:T(8,128)S(1)} %get-tuple-element.11), channel_id=1, replica_groups=mesh['dom'=4,'bulk'=8] {'bulk'}, dimensions={0} | all-to-all | bytes 983040 | tf_op jit(solution)/shard_map/all_to_all | solution.py:396
  23.8 16.7 %project.1 = f32[1472,128]{1,0:T(8,128)S(1)} custom-call(f32[960,128]{1,0:T(8,128)S(1)} %bitcast.7, f32[20032,128]{1,0:T(8,128)S(1)} %get-tuple-element.12.net_ref), custom_call_target="tpu_custom_call" | custom-call | tf_op jit(solution)/shard_map/project/pallas_call | solution.py:325
  40.5 14.6 %all_to_all.11 = f32[8,184,128]{2,1,0:T(8,128)S(1)} all-to-all(f32[8,184,128]{2,1,0:T(8,128)S(1)} %bitcast.6), channel_id=1, replica_groups=mesh['dom'=4,'bulk'=8] {'bulk'}, dimensions={0} | all-to-all | bytes 1507328 | tf_op jit(solution)/shard_map/all_to_all | solution.py:398
  55.1 5.8 %give_back.1 = f32[9,16384]{1,0:T(8,128)} custom-call(s32[128,128]{1,0:T(8,128)S(1)} %get-tuple-element.9.key_ref, s32[8,128]{1,0:T(8,128)S(1)} %get-tuple-element.10.first_smem, f32[1472,128]{1,0:T(8,128)S(1)} %bitcast.5), custom_call_target="tpu_custom_call" | custom-call | tf_op jit(solution)/shard_map/give_back/pallas_call | solution.py:377

commit v4 on v3

--- a/solution.py
+++ b/solution.py
@@ -31,16 +31,18 @@
 
 
 def route_kernel(owners, windows, patch_dev, patch_hbm, span_hbm, grid_hbm, target_hbm, net_hbm,
-                 sent_ref, key_ref, first_ref, net_ref,
-                 patch_ref, span_ref, grid_ref, target_ref,
-                 code_ref, load_ref, slot_ref, first_smem, in_sem, net_sem, first_sem):
+                 *refs):
+    sent_refs = refs[:owners // 2]
+    (key_ref, first_ref, net_ref, patch_ref, span_ref, grid_ref, target_ref,
+     code_ref, load_ref, slot_ref, first_smem, in_sem, net_sem, first_sem) = refs[owners // 2:]
+    me = lax.axis_index("bulk")
     copies = []
     for k, (source, to) in enumerate(
             ((patch_hbm, patch_ref), (span_hbm, span_ref), (grid_hbm, grid_ref), (target_hbm, target_ref))):
         copies.append(pltpu.make_async_copy(source, to, in_sem.at[k]))
         copies[-1].start()
     chunks = net_hbm.shape[1] // LANES
-    patch_pad = net_ref.shape[0] // chunks
+    patch_pad = net_ref.shape[0] // (2 * chunks)
     loads = []
     for c in range(chunks):
         loads.append(pltpu.make_async_copy(
@@ -53,6 +55,8 @@
     owner = jnp.zeros_like(patch)
     for o in range(1, owners):
         owner += (patch >= o * patch_dev).astype(jnp.int32)
+    local = patch - owner * patch_dev
+    owner = owner ^ me
 
     lane = iota((LANES, LANES), 1)
     sub = iota((LANES, LANES), 0)
@@ -64,18 +68,22 @@
     diagonal = iota((blocks, blocks), 0) == iota((blocks, blocks), 1)
 
     key = jnp.zeros_like(patch)
-    for o in range(owners):
-        mine = owner == o
-        mask = mine.astype(jnp.bfloat16)
-        counts = jnp.dot(mask, counter, preferred_element_type=jnp.float32)
+    found = []
+    for x in range(owners):
+        mine = owner == x
+        counts = jnp.dot(mine.astype(jnp.bfloat16), counter, preferred_element_type=jnp.float32)
         total = counts[:, LANES:]
-        offset = jnp.dot(earlier, total.astype(jnp.bfloat16), preferred_element_type=jnp.float32).astype(jnp.int32)
+        offset = jnp.dot(earlier, total.astype(jnp.bfloat16), preferred_element_type=jnp.float32)
+        first = jnp.sum(jnp.where(diagonal, offset, 0.0), axis=0, keepdims=True)
+        first_ref[x:x + 1, :] = first.astype(jnp.int32) >> 7
         before = counts[:, :LANES].astype(jnp.int32) - mine.astype(jnp.int32)
-        total = total.astype(jnp.int32)
-        edge = offset & (LANES - 1)
-        key = jnp.where(mine, before + edge + 2 * LANES * o, key)
-        first = jnp.sum(jnp.where(diagonal, offset.astype(jnp.float32), 0.0), axis=0, keepdims=True)
-        first_ref[o:o + 1, :] = first.astype(jnp.int32) >> 7
+        edge = offset.astype(jnp.int32) & (LANES - 1)
+        key = jnp.where(mine, before + edge + 2 * LANES * x, key)
+        found.append((mine, before, edge, total.astype(jnp.int32)))
+    copy = pltpu.make_async_copy(first_ref, first_smem, first_sem)
+    copy.start()
+    for x in range(owners):
+        mine, before, edge, total = found[x]
         word = jnp.where(mine, blane + LANES * (blane - before), 0)
         for bit in range(7):
             moves = 1 << (7 + bit)
@@ -84,15 +92,13 @@
         rank = (blane - edge) & (LANES - 1)
         source = take_lanes(word & (LANES - 1), rank)
         valid = rank < total
-        code_ref[o * blocks:(o + 1) * blocks, :] = source + jnp.where(valid, jnp.where(blane >= edge, 128, 256), 0)
+        code_ref[x * blocks:(x + 1) * blocks, :] = source + jnp.where(valid, jnp.where(blane >= edge, 128, 256), 0)
 
     key_ref[...] = key
-    copy = pltpu.make_async_copy(first_ref, first_smem, first_sem)
-    copy.start()
     for waiting in copies[1:]:
         waiting.wait()
     span = span_ref[...]
-    row = (2 * ((span >> 1) * patch_pad + patch - owner * patch_dev) + (span & 1)).astype(jnp.float32)
+    row = (2 * ((span >> 1) * patch_pad + local) + (span & 1)).astype(jnp.float32)
     for b in range(blocks):
         load_ref[8 * b:8 * b + 3, :] = target_ref[:, b * LANES:(b + 1) * LANES]
         load_ref[8 * b + 3:8 * b + 5, :] = (grid_ref[:, b * LANES:(b + 1) * LANES].astype(jnp.float32) + 0.5) * (1.0 / LEVELS)
@@ -113,12 +119,13 @@
 
     lax.fori_loop(0, blocks // UNROLL, place, 0)
 
-    for o in range(owners):
+    for x in range(owners):
         for c in range(SENT):
             for w in range(0, windows, 8):
                 size = min(8, windows - w)
-                rows = slot_ref[pl.ds((o * (windows + 1) + w) * 8 + c, size, stride=8), :]
-                sent_ref[o, c * windows + w:c * windows + w + size, :] = rows
+                rows = slot_ref[pl.ds((x * (windows + 1) + w) * 8 + c, size, stride=8), :]
+                at = ((x % 2) * SENT + c) * windows + w
+                sent_refs[x // 2][at:at + size, :] = rows
     for waiting in loads:
         waiting.wait()
 
@@ -132,13 +139,13 @@
     return pl.pallas_call(
         functools.partial(route_kernel, owners, windows, patch_dev),
         out_shape=(
-            jax.ShapeDtypeStruct((owners, SENT * windows, LANES), jnp.float32),
+            *[jax.ShapeDtypeStruct((2 * SENT * windows, LANES), jnp.float32)] * (owners // 2),
             jax.ShapeDtypeStruct((blocks, LANES), jnp.int32),
             jax.ShapeDtypeStruct((owners, blocks), jnp.int32),
-            jax.ShapeDtypeStruct((chunks * patch_pad, LANES), jnp.float32),
+            jax.ShapeDtypeStruct((2 * chunks * patch_pad, LANES), jnp.float32),
         ),
         in_specs=[pl.BlockSpec(memory_space=pltpu.HBM)] * 5,
-        out_specs=[pl.BlockSpec(memory_space=pltpu.VMEM)] * 4,
+        out_specs=[pl.BlockSpec(memory_space=pltpu.VMEM)] * (owners // 2 + 3),
         scratch_shapes=[
             pltpu.VMEM((blocks, LANES), jnp.int32),
             pltpu.VMEM((blocks, LANES), jnp.int32),
@@ -226,22 +233,30 @@
 PROJECT_STEPS = ITERS * 27 + 25
 
 
-def project_kernel(sources, windows, given_pad, got_ref, net_ref, out_ref,
-                   index_ref, index_0, index_1, index_2, index_3, tile_even, tile_odd, coeff_even, coeff_odd, index_sem):
-    groups = sources // 8
-    sent = SENT * windows
-    total = windows * groups
+def project_kernel(pairs, windows, given_pad, *refs):
+    got_refs, (_, other_ref), out_refs = refs[:pairs], refs[pairs:pairs + 2], refs[pairs + 2:2 * pairs + 2]
+    (net_ref, load_ref, index_ref, index_0, index_1, index_2, index_3,
+     tile_even, tile_odd, coeff_even, coeff_odd, index_sem, net_sem) = refs[2 * pairs + 2:]
+    per = 8 // pairs
+    half = windows // per
+    total = 2 * half
+    rows = net_ref.shape[0] // 2
     indices = (index_0, index_1, index_2, index_3)
     tiles, coeffs = (tile_even, tile_odd), (coeff_even, coeff_odd)
     depth = len(indices)
+    patches, chunks = other_ref.shape[0], other_ref.shape[1] // LANES
+    patch_pad = rows // chunks
 
     def arrived(t, c):
-        w, g = t // groups, t % groups
-        return got_ref[pl.ds(g * 8 * sent + c * windows + w, 8, stride=sent), :]
+        return load_ref[pl.ds(pl.multiple_of((t * SENT + c) * 8, 8), 8), :]
 
     def fetch(t, k):
         return pltpu.make_async_copy(
             index_ref.at[pl.ds(pl.multiple_of(8 * t, 8), 8), :], indices[k % depth], index_sem.at[k % depth])
+
+    def partner(c):
+        return pltpu.make_async_copy(
+            other_ref.at[:, pl.ds(c * LANES, LANES)], net_ref.at[pl.ds(rows + c * patch_pad, patches), :], net_sem.at[c])
 
     def gather(k):
         index, tile = indices[k % depth], tiles[k % 2]
@@ -260,10 +275,11 @@
 
     def solve(t, k):
         def finish(result):
-            w, g = t // groups, t % groups
+            base = t // half * given_pad + t % half * per
             for c in range(GIVEN):
                 at = (c + 1) % GIVEN
-                out_ref[pl.ds(g * 8 * given_pad + at * windows + w, 8, stride=given_pad), :] = result[c]
+                for j in range(pairs):
+                    out_refs[j][pl.ds(base + at * windows, per), :] = result[c][j * per:(j + 1) * per, :]
 
         return project(
             lambda e: coeffs[k % 2][8 * e:8 * e + 8, :],
@@ -288,10 +304,22 @@
     def solving(t, k):
         return solve(t, k), PROJECT_STEPS
 
+    def collect(t, c):
+        at = (t // half * SENT + c) * windows + t % half * per
+        for j in range(pairs):
+            to = (t * SENT + c) * 8 + j * per
+            load_ref[to:to + per, :] = got_refs[j][at:at + per, :]
+
     for t in range(total):
-        index_ref[8 * t:8 * t + 8, :] = arrived(t, 5).astype(jnp.int32) >> 1
+        collect(t, SENT - 1)
+        index_ref[8 * t:8 * t + 8, :] = (arrived(t, SENT - 1).astype(jnp.int32) >> 1) + t // half * rows
         if t < depth:
             fetch(t, t).start()
+    for c in range(chunks):
+        partner(c).start()
+    for t in range(total):
+        for c in range(SENT - 1):
+            collect(t, c)
     index_ref[8 * total:8 * total + 8, :] = jnp.zeros((8, LANES), jnp.int32)
     fetch(0, 0).wait()
     interleave(gathering(0))
@@ -300,6 +328,11 @@
     interleave(gathering(1), turning(0, 0))
 
     def steps(i, carry):
+        @pl.when(i == -(-(half - depth - 1) // depth))
+        def _():
+            for c in range(chunks):
+                partner(c).wait()
+
         for k in range(depth):
             t = depth * i + k
             fetch(t + 2, k + 2).wait()
@@ -319,15 +352,21 @@
     fetch(total, total).wait()
 
 
-def project_nodes(got, net, windows, given_pad):
-    sources = got.shape[0]
-    tiles = windows * sources
+def project_nodes(got, net_rows, other, windows, given_pad):
+    pairs = len(got)
+    chunks = other.shape[1] // LANES
+    tiles = 2 * pairs * windows
     return pl.pallas_call(
-        functools.partial(project_kernel, sources, windows, given_pad),
-        out_shape=jax.ShapeDtypeStruct((sources * given_pad, LANES), jnp.float32),
-        in_specs=[pl.BlockSpec(memory_space=pltpu.VMEM)] * 2,
-        out_specs=pl.BlockSpec(memory_space=pltpu.VMEM),
+        functools.partial(project_kernel, pairs, windows, given_pad),
+        out_shape=(
+            *[jax.ShapeDtypeStruct((2 * given_pad, LANES), jnp.float32)] * pairs,
+            jax.ShapeDtypeStruct(net_rows.shape, jnp.float32),
+        ),
+        in_specs=[pl.BlockSpec(memory_space=pltpu.VMEM)] * (pairs + 1) + [pl.BlockSpec(memory_space=pl.ANY)],
+        out_specs=[pl.BlockSpec(memory_space=pltpu.VMEM)] * (pairs + 1),
+        input_output_aliases={pairs: pairs},
         scratch_shapes=[
+            pltpu.VMEM((tiles * SENT, LANES), jnp.float32),
             pltpu.VMEM((tiles + 8, LANES), jnp.int32),
             pltpu.SMEM((8, LANES), jnp.int32),
             pltpu.SMEM((8, LANES), jnp.int32),
@@ -338,13 +377,15 @@
             pltpu.VMEM((64 * 8, LANES), jnp.float32),
             pltpu.VMEM((64 * 8, LANES), jnp.float32),
             pltpu.SemaphoreType.DMA((4,)),
+            pltpu.SemaphoreType.DMA((chunks,)),
         ],
-        compiler_params=pltpu.CompilerParams(vmem_limit_bytes=24 * 2**20),
+        compiler_params=pltpu.CompilerParams(vmem_limit_bytes=12 * 2**20),
         name="project",
-    )(got.reshape(sources * SENT * windows, LANES), net)
-
-
-def return_kernel(owners, windows, given_pad, key_ref, first_smem, got_ref, out_ref):
+    )(*got, net_rows, other)[:pairs]
+
+
+def return_kernel(owners, windows, given_pad, key_ref, first_smem, *refs):
+    got_refs, out_ref = refs[:-1], refs[-1]
     blocks = key_ref.shape[0]
     sub = iota((8, LANES), 0)
 
@@ -357,13 +398,14 @@
             rest = jnp.where(sub < 2, key - sub, -1)
             main = jnp.zeros((8, LANES), jnp.float32)
             last = jnp.zeros((8, LANES), jnp.float32)
-            for o in range(owners):
-                base = o * given_pad + first_smem[o, b]
+            for x in range(owners):
+                got_ref = got_refs[x // 2]
+                base = (x % 2) * given_pad + first_smem[x, b]
                 moved = take_lanes(got_ref[pl.ds(base, 8), :], lane)
-                last = jnp.where(rest == 2 * o, moved, last)
+                last = jnp.where(rest == 2 * x, moved, last)
                 for step_over in range(2):
                     rows = got_ref[pl.ds(base + windows + step_over, 8, stride=windows), :]
-                    main = jnp.where(key == 2 * o + step_over, take_lanes(rows, lane), main)
+                    main = jnp.where(key == 2 * x + step_over, take_lanes(rows, lane), main)
             at = pl.ds(pl.multiple_of(b * LANES, LANES), LANES)
             out_ref[0:8, at] = main
             out_ref[8:9, at] = jnp.sum(last, axis=0, keepdims=True)
@@ -380,24 +422,27 @@
         in_specs=[
             pl.BlockSpec(memory_space=pltpu.VMEM),
             pl.BlockSpec(memory_space=pltpu.SMEM),
-            pl.BlockSpec(memory_space=pltpu.VMEM),
-        ],
+        ] + [pl.BlockSpec(memory_space=pltpu.VMEM)] * len(got),
         out_specs=pl.BlockSpec(memory_space=pltpu.VMEM),
         compiler_params=pltpu.CompilerParams(vmem_limit_bytes=16 * 2**20),
         name="give_back",
-    )(key, first, got.reshape(owners * given_pad, LANES))
+    )(key, first, *got)
 
 
 def body(node_patch, node_span, start_grid, target, net):
     owners = lax.axis_size("bulk")
     windows = node_patch.shape[0] * 5 // 32 // LANES
     given_pad = round_up(GIVEN * windows + 1, 8)
-    sent, key, first, net_rows = route(node_patch, node_span, start_grid, target, net, owners, windows)
-    got = lax.all_to_all(sent, "bulk", split_axis=0, concat_axis=0, tiled=True)
-    placed = project_nodes(got, net_rows, windows, given_pad)
-    answered = lax.all_to_all(
-        placed.reshape(owners, given_pad, LANES), "bulk", split_axis=0, concat_axis=0, tiled=True)
-    return return_nodes(key, first, answered, windows, given_pad)
+    def swap(value, distance):
+        return lax.ppermute(value, "bulk", [(i, i ^ distance) for i in range(owners)])
+
+    def swap_pairs(values):
+        return [swap(value, 2 * j) if j else value for j, value in enumerate(values)]
+
+    other = swap(net, 1)
+    *sent, key, first, net_rows = route(node_patch, node_span, start_grid, target, net, owners, windows)
+    placed = project_nodes(swap_pairs(sent), net_rows, other, windows, given_pad)
+    return return_nodes(key, first, swap_pairs(placed), windows, given_pad)
 
 
 def solution(mesh):

time: 61.1 us -> 55.9 us (0.915)
  blocking collectives: 29 us -> 0 us
  waiting for transfers between devices: 0 us -> 14.4 us
  starting transfers between devices: 0 us -> 8.1 us
  Pallas kernels: 31.9 us -> 33.2 us
    all_to_all x2 -> x0, blocking collectives: 29 us -> none  [the longest x1 14.6 us: body(): lax.all_to_all(placed.reshape(owners, given_pad, LANES), 'bulk', split_ax...]
    ppermute x0 -> x7, waiting for transfers between devices: none -> 14.4 us  [swap(): lax.ppermute(value, 'bulk', [(i, i ^ distance) for i in range(owners)])]
    ppermute x0 -> x7, starting transfers between devices: none -> 8.1 us  [swap(): lax.ppermute(value, 'bulk', [(i, i ^ distance) for i in range(owners)])]
    pallas_call x1, Pallas kernels: 16.7 us -> 18 us  [project_nodes(): pl.pallas_call(functools.partial(project_kernel, pairs, windows, given_pa...]
  transfers between devices with their start and end apart: 0 -> 7, of which waited for: 0 -> 4; matrix products, arithmetic and copies ran while one was open for 0% -> 0% of each run, Pallas kernels for 0% -> 17%
where the time goes in v4:
time: 55.9 us; the launch traced here: 55.7 us
  Pallas kernels  33.2 us (59%)
  waiting for transfers between devices  14.4 us (26%)
  starting transfers between devices  8.1 us (14%)
    pallas_call x1, Pallas kernels, project_nodes(): pl.pallas_call(functools.partial(project_kernel, pairs, windows, given_pa...  18 us
    ppermute x7, waiting for transfers between devices, swap(): lax.ppermute(value, 'bulk', [(i, i ^ distance) for i in range(owners)])  14.4 us
    pallas_call x1, Pallas kernels, route(): pl.pallas_call(functools.partial(route_kernel, owners, windows, patch_dev...  9.42 us
    ppermute x7, starting transfers between devices, swap(): lax.ppermute(value, 'bulk', [(i, i ^ distance) for i in range(owners)])  8.1 us
    pallas_call x1, Pallas kernels, return_nodes(): pl.pallas_call(functools.partial(return_kernel, owners, windows, given_pa...  5.78 us
  transfers between devices with their start and end apart: 7, of which 4 were waited for; matrix products, arithmetic and copies ran while one was open for 0% of the time, Pallas kernels for 17%

profile of v4, /device:TPU:0, one launch (start us, length us, event | category | flops | bytes accessed | tf_op | source)
XLA Modules:
  0.0 55.7 jit_solution(11239028347668546906)
XLA Ops:
  0.0 0.5 collective-permute-start.3
  0.5 9.4 %route.1 = (f32[240,128]{1,0:T(8,128)S(1)}, f32[240,128]{1,0:T(8,128)S(1)}, f32[240,128]{1,0:T(8,128)S(1)}, f32[240,128]{1,0:T(8,128)S(1)}, s32[128,128]{1,0:T(8...) custom-call(s32[128,128]{1,0:T(8,128)} %bitcast.2, s32[128,128]{1,0:T(8,128)} %bitcast.3, s32[2,16384]{1,0:T(2,128)} %grid_hbm.1, ...), custom_call_target="tpu_custom_call" | custom-call | tf_op jit(solution)/shard_map/route/pallas_call | solution.py:139
  9.9 2.6 %collective-permute-start = (f32[240,128]{1,0:T(8,128)S(1)}, f32[240,128]{1,0:T(8,128)S(1)}, u32[]{:S(2)}, u32[]{:S(2)}) collective-permute-start(f32[240,128]{1,0:T(8,128)S(1)} %get-tuple-element.19), channel_id=1, source_target_pairs={{0,2},{1,3},{2,0},{3,1},{4,6},{5,7},{6,4},{7,5},{8,10},{9,11},{10,... | collective-permute-start | bytes 368648 | tf_op jit(solution)/shard_map/ppermute | solution.py:437
  12.4 1.5 %collective-permute-start.1 = (f32[240,128]{1,0:T(8,128)S(1)}, f32[240,128]{1,0:T(8,128)S(1)}, u32[]{:S(2)}, u32[]{:S(2)}) collective-permute-start(f32[240,128]{1,0:T(8,128)S(1)} %get-tuple-element.20), channel_id=1, source_target_pairs={{0,4},{1,5},{2,6},{3,7},{4,0},{5,1},{6,2},{7,3},{8,12},{9,13},{10,... | collective-permute-start | bytes 368648 | tf_op jit(solution)/shard_map/ppermute | solution.py:437
  14.0 0.0 collective-permute-start.2
  14.0 2.5 %collective-permute-done.refs_1_ = f32[240,128]{1,0:T(8,128)S(1)} collective-permute-done((f32[240,128]{1,0:T(8,128)S(1)}, f32[240,128]{1,0:T(8,128)S(1)}, u32[]{:S(2)}, u32[]{:S(2)}) %collective-permute-start) | collective-permute-done | bytes 122912 | tf_op jit(solution)/shard_map/ppermute | solution.py:437
  16.4 4.1 %collective-permute-done.1.refs_2_ = f32[240,128]{1,0:T(8,128)S(1)} collective-permute-done((f32[240,128]{1,0:T(8,128)S(1)}, f32[240,128]{1,0:T(8,128)S(1)}, u32[]{:S(2)}, u32[]{:S(2)}) %collective-permute-start.1) | collective-permute-done | bytes 122912 | tf_op jit(solution)/shard_map/ppermute | solution.py:437
  20.5 0.0 collective-permute-done.2.refs_3_
  20.5 0.0 collective-permute-done.3.refs_5_
  20.5 18.0 %project.1 = (f32[368,128]{1,0:T(8,128)S(1)}, f32[368,128]{1,0:T(8,128)S(1)}, f32[368,128]{1,0:T(8,128)S(1)}, f32[368,128]{1,0:T(8,128)S(1)}, f32[40064,128]{1,0:T(8,128)S(1)}) custom-call(f32[240,128]{1,0:T(8,128)S(1)} %get-tuple-element.18.refs_0_, f32[240,128]{1,0:T(8,128)S(1)} %collective-permute-done.refs_1_, ...), custom_call_target="tpu_custom_call", output_to_operand_aliasing={{4}: (4, {})} | custom-call | tf_op jit(solution)/shard_map/project/pallas_call | solution.py:359
  38.6 1.3 %collective-permute-start.4 = (f32[368,128]{1,0:T(8,128)S(1)}, f32[368,128]{1,0:T(8,128)S(1)}, u32[]{:S(2)}, u32[]{:S(2)}) collective-permute-start(f32[368,128]{1,0:T(8,128)S(1)} %get-tuple-element.24), channel_id=1, source_target_pairs={{0,2},{1,3},{2,0},{3,1},{4,6},{5,7},{6,4},{7,5},{8,10},{9,11},{10,... | collective-permute-start | bytes 565256 | tf_op jit(solution)/shard_map/ppermute | solution.py:437
  39.9 0.9 %collective-permute-start.5 = (f32[368,128]{1,0:T(8,128)S(1)}, f32[368,128]{1,0:T(8,128)S(1)}, u32[]{:S(2)}, u32[]{:S(2)}) collective-permute-start(f32[368,128]{1,0:T(8,128)S(1)} %get-tuple-element.25), channel_id=1, source_target_pairs={{0,4},{1,5},{2,6},{3,7},{4,0},{5,1},{6,2},{7,3},{8,12},{9,13},{10,... | collective-permute-start | bytes 565256 | tf_op jit(solution)/shard_map/ppermute | solution.py:437
  40.7 1.4 %collective-permute-start.6 = (f32[368,128]{1,0:T(8,128)S(1)}, f32[368,128]{1,0:T(8,128)S(1)}, u32[]{:S(2)}, u32[]{:S(2)}) collective-permute-start(f32[368,128]{1,0:T(8,128)S(1)} %get-tuple-element.26), channel_id=1, source_target_pairs={{0,6},{1,7},{2,4},{3,5},{4,2},{5,3},{6,0},{7,1},{8,14},{9,15},{10,... | collective-permute-start | bytes 565256 | tf_op jit(solution)/shard_map/ppermute | solution.py:437
  42.1 3.8 %collective-permute-done.4.refs_1_ = f32[368,128]{1,0:T(8,128)S(1)} collective-permute-done((f32[368,128]{1,0:T(8,128)S(1)}, f32[368,128]{1,0:T(8,128)S(1)}, u32[]{:S(2)}, u32[]{:S(2)}) %collective-permute-start.4) | collective-permute-done | bytes 188448 | tf_op jit(solution)/shard_map/ppermute | solution.py:437
  45.9 4.1 %collective-permute-done.5.refs_2_ = f32[368,128]{1,0:T(8,128)S(1)} collective-permute-done((f32[368,128]{1,0:T(8,128)S(1)}, f32[368,128]{1,0:T(8,128)S(1)}, u32[]{:S(2)}, u32[]{:S(2)}) %collective-permute-start.5) | collective-permute-done | bytes 188448 | tf_op jit(solution)/shard_map/ppermute | solution.py:437
  50.0 0.0 collective-permute-done.6.refs_3_
  50.0 5.8 %give_back.1 = f32[9,16384]{1,0:T(8,128)} custom-call(s32[128,128]{1,0:T(8,128)S(1)} %get-tuple-element.16.key_ref, s32[8,128]{1,0:T(8,128)S(1)} %get-tuple-element.17.first_smem, f32[368,128]{1,0:T(8,128)S(1)} %get-tuple-element.23.refs_0_, f32[368,128]{1,0:T(8,128)S(1)} %collective-permute-done.4.refs_1_, f32[368,128]{1,0:T(8,128)S(1)} %collective-permute-done.5.refs_2_, ...), custom_call_target="tpu_custom_call" | custom-call | tf_op jit(solution)/shard_map/give_back/pallas_call | solution.py:419
Async XLA Ops:
  0.0 20.5 %collective-permute-start.3 = (f32[2500,1024]{1,0:T(8,128)}, f32[2500,1024]{1,0:T(8,128)S(1)}, u32[]{:S(2)}, u32[]{:S(2)}) collective-permute-start(f32[2500,1024]{1,0:T(8,128)} %net_hbm.1), channel_id=1, source_target_pairs={{0,1},{1,0},{2,3},{3,2},{4,5},{5,4},{6,7},{7,6},{8,9},{9,8},{10,11... | collective-permute-start | bytes 30720008 | tf_op jit(solution)/shard_map/ppermute | solution.py:437
  9.9 6.5 %collective-permute-start = (f32[240,128]{1,0:T(8,128)S(1)}, f32[240,128]{1,0:T(8,128)S(1)}, u32[]{:S(2)}, u32[]{:S(2)}) collective-permute-start(f32[240,128]{1,0:T(8,128)S(1)} %get-tuple-element.19), channel_id=1, source_target_pairs={{0,2},{1,3},{2,0},{3,1},{4,6},{5,7},{6,4},{7,5},{8,10},{9,11},{10,... | collective-permute-start | bytes 368648 | tf_op jit(solution)/shard_map/ppermute | solution.py:437
  12.4 8.1 %collective-permute-start.1 = (f32[240,128]{1,0:T(8,128)S(1)}, f32[240,128]{1,0:T(8,128)S(1)}, u32[]{:S(2)}, u32[]{:S(2)}) collective-permute-start(f32[240,128]{1,0:T(8,128)S(1)} %get-tuple-element.20), channel_id=1, source_target_pairs={{0,4},{1,5},{2,6},{3,7},{4,0},{5,1},{6,2},{7,3},{8,12},{9,13},{10,... | collective-permute-start | bytes 368648 | tf_op jit(solution)/shard_map/ppermute | solution.py:437
  14.0 6.6 %collective-permute-start.2 = (f32[240,128]{1,0:T(8,128)S(1)}, f32[240,128]{1,0:T(8,128)S(1)}, u32[]{:S(2)}, u32[]{:S(2)}) collective-permute-start(f32[240,128]{1,0:T(8,128)S(1)} %get-tuple-element.21), channel_id=1, source_target_pairs={{0,6},{1,7},{2,4},{3,5},{4,2},{5,3},{6,0},{7,1},{8,14},{9,15},{10,... | collective-permute-start | bytes 368648 | tf_op jit(solution)/shard_map/ppermute | solution.py:437
  38.6 7.3 %collective-permute-start.4 = (f32[368,128]{1,0:T(8,128)S(1)}, f32[368,128]{1,0:T(8,128)S(1)}, u32[]{:S(2)}, u32[]{:S(2)}) collective-permute-start(f32[368,128]{1,0:T(8,128)S(1)} %get-tuple-element.24), channel_id=1, source_target_pairs={{0,2},{1,3},{2,0},{3,1},{4,6},{5,7},{6,4},{7,5},{8,10},{9,11},{10,... | collective-permute-start | bytes 565256 | tf_op jit(solution)/shard_map/ppermute | solution.py:437
  39.9 10.1 %collective-permute-start.5 = (f32[368,128]{1,0:T(8,128)S(1)}, f32[368,128]{1,0:T(8,128)S(1)}, u32[]{:S(2)}, u32[]{:S(2)}) collective-permute-start(f32[368,128]{1,0:T(8,128)S(1)} %get-tuple-element.25), channel_id=1, source_target_pairs={{0,4},{1,5},{2,6},{3,7},{4,0},{5,1},{6,2},{7,3},{8,12},{9,13},{10,... | collective-permute-start | bytes 565256 | tf_op jit(solution)/shard_map/ppermute | solution.py:437
  40.7 9.2 %collective-permute-start.6 = (f32[368,128]{1,0:T(8,128)S(1)}, f32[368,128]{1,0:T(8,128)S(1)}, u32[]{:S(2)}, u32[]{:S(2)}) collective-permute-start(f32[368,128]{1,0:T(8,128)S(1)} %get-tuple-element.26), channel_id=1, source_target_pairs={{0,6},{1,7},{2,4},{3,5},{4,2},{5,3},{6,0},{7,1},{8,14},{9,15},{10,... | collective-permute-start | bytes 565256 | tf_op jit(solution)/shard_map/ppermute | solution.py:437

commit v5 on v4

--- a/solution.py
+++ b/solution.py
@@ -47,7 +47,8 @@
     for c in range(chunks):
         loads.append(pltpu.make_async_copy(
             net_hbm.at[:, pl.ds(c * LANES, LANES)], net_ref.at[pl.ds(c * patch_pad, patch_dev), :], net_sem.at[c]))
-        loads[-1].start()
+    for load in loads[:chunks // 2]:
+        load.start()
     slot_ref[...] = jnp.zeros_like(slot_ref)
     blocks = patch_ref.shape[0]
     copies[0].wait()
@@ -82,6 +83,8 @@
         found.append((mine, before, edge, total.astype(jnp.int32)))
     copy = pltpu.make_async_copy(first_ref, first_smem, first_sem)
     copy.start()
+    for load in loads[chunks // 2:]:
+        load.start()
     for x in range(owners):
         mine, before, edge, total = found[x]
         word = jnp.where(mine, blane + LANES * (blane - before), 0)
@@ -236,13 +239,13 @@
 def project_kernel(pairs, windows, given_pad, *refs):
     got_refs, (_, other_ref), out_refs = refs[:pairs], refs[pairs:pairs + 2], refs[pairs + 2:2 * pairs + 2]
     (net_ref, load_ref, index_ref, index_0, index_1, index_2, index_3,
-     tile_even, tile_odd, coeff_even, coeff_odd, index_sem, net_sem) = refs[2 * pairs + 2:]
+     tile_even, tile_odd, turn_even, turn_odd, coeff_ref, index_sem, net_sem) = refs[2 * pairs + 2:]
     per = 8 // pairs
     half = windows // per
     total = 2 * half
     rows = net_ref.shape[0] // 2
     indices = (index_0, index_1, index_2, index_3)
-    tiles, coeffs = (tile_even, tile_odd), (coeff_even, coeff_odd)
+    tiles, turns = (tile_even, tile_odd), (turn_even, turn_odd)
     depth = len(indices)
     patches, chunks = other_ref.shape[0], other_ref.shape[1] // LANES
     patch_pad = rows // chunks
@@ -265,15 +268,24 @@
                 tile[s * LANES + i:s * LANES + i + 1, :] = net_ref[pl.ds(index[s, i], 1), :]
                 yield
 
-    def turn(t, k):
-        tile, coeff = tiles[k % 2], coeffs[k % 2]
-        odd = (arrived(t, 5).astype(jnp.int32) & 1) == 1
+    def turn(k):
+        tile, turned = tiles[k % 2], turns[k % 2]
         for s in range(8):
-            both = tile[s * LANES:(s + 1) * LANES, :].T
-            coeff[pl.ds(s, 64, stride=8), :] = jnp.where(odd[s:s + 1, :], both[64:, :], both[:64, :])
+            turned[pl.ds(s, LANES, stride=8), :] = tile[s * LANES:(s + 1) * LANES, :].T
             yield
 
     def solve(t, k):
+        turned = turns[k % 2]
+        odd = (arrived(t, SENT - 1).astype(jnp.int32) & 1) == 1
+        kept = set()
+
+        def read(e):
+            at = slice(8 * e, 8 * e + 8)
+            if e not in kept:
+                kept.add(e)
+                coeff_ref[at, :] = jnp.where(odd, turned[512 + 8 * e:520 + 8 * e, :], turned[at, :])
+            return coeff_ref[at, :]
+
         def finish(result):
             base = t // half * given_pad + t % half * per
             for c in range(GIVEN):
@@ -282,7 +294,7 @@
                     out_refs[j][pl.ds(base + at * windows, per), :] = result[c][j * per:(j + 1) * per, :]
 
         return project(
-            lambda e: coeffs[k % 2][8 * e:8 * e + 8, :],
+            read,
             lambda: [arrived(t, c) for c in range(3)],
             lambda: (arrived(t, 3), arrived(t, 4)),
             finish)
@@ -298,8 +310,8 @@
     def gathering(k):
         return gather(k), 8 * LANES
 
-    def turning(t, k):
-        return turn(t, k), 8
+    def turning(k):
+        return turn(k), 8
 
     def solving(t, k):
         return solve(t, k), PROJECT_STEPS
@@ -320,12 +332,13 @@
     for t in range(total):
         for c in range(SENT - 1):
             collect(t, c)
-    index_ref[8 * total:8 * total + 8, :] = jnp.zeros((8, LANES), jnp.int32)
+    index_ref[8 * total:8 * total + 16, :] = jnp.zeros((16, LANES), jnp.int32)
     fetch(0, 0).wait()
     interleave(gathering(0))
+    fetch(depth, depth).start()
     fetch(1, 1).wait()
-    fetch(depth, depth).start()
-    interleave(gathering(1), turning(0, 0))
+    interleave(gathering(1), turning(0))
+    fetch(depth + 1, depth + 1).start()
 
     def steps(i, carry):
         @pl.when(i == -(-(half - depth - 1) // depth))
@@ -336,20 +349,21 @@
         for k in range(depth):
             t = depth * i + k
             fetch(t + 2, k + 2).wait()
-            fetch(t + depth + 1, k + 1).start()
-            interleave(gathering(k + 2), turning(t + 1, k + 1), solving(t, k))
+            interleave(gathering(k + 2), turning(k + 1), solving(t, k))
+            fetch(t + depth + 2, k + 2).start()
         return carry
 
     lax.fori_loop(0, total // depth - 1, steps, 0)
     for t in range(total - depth, total):
         if t + 2 < total:
             fetch(t + 2, t + 2).wait()
-            interleave(gathering(t + 2), turning(t + 1, t + 1), solving(t, t))
+            interleave(gathering(t + 2), turning(t + 1), solving(t, t))
         elif t + 1 < total:
-            interleave(turning(t + 1, t + 1), solving(t, t))
+            interleave(turning(t + 1), solving(t, t))
         else:
             interleave(solving(t, t))
-    fetch(total, total).wait()
+    for t in (total, total + 1):
+        fetch(t, t).wait()
 
 
 def project_nodes(got, net_rows, other, windows, given_pad):
@@ -367,14 +381,15 @@
         input_output_aliases={pairs: pairs},
         scratch_shapes=[
             pltpu.VMEM((tiles * SENT, LANES), jnp.float32),
-            pltpu.VMEM((tiles + 8, LANES), jnp.int32),
+            pltpu.VMEM((tiles + 16, LANES), jnp.int32),
             pltpu.SMEM((8, LANES), jnp.int32),
             pltpu.SMEM((8, LANES), jnp.int32),
             pltpu.SMEM((8, LANES), jnp.int32),
             pltpu.SMEM((8, LANES), jnp.int32),
             pltpu.VMEM((8 * LANES, LANES), jnp.float32),
             pltpu.VMEM((8 * LANES, LANES), jnp.float32),
-            pltpu.VMEM((64 * 8, LANES), jnp.float32),
+            pltpu.VMEM((8 * LANES, LANES), jnp.float32),
+            pltpu.VMEM((8 * LANES, LANES), jnp.float32),
             pltpu.VMEM((64 * 8, LANES), jnp.float32),
             pltpu.SemaphoreType.DMA((4,)),
             pltpu.SemaphoreType.DMA((chunks,)),
@@ -385,7 +400,7 @@
 
 
 def return_kernel(owners, windows, given_pad, key_ref, first_smem, *refs):
-    got_refs, out_ref = refs[:-1], refs[-1]
+    got_refs, (out_hbm, out_ref, out_sem) = refs[:-3], refs[-3:]
     blocks = key_ref.shape[0]
     sub = iota((8, LANES), 0)
 
@@ -411,7 +426,16 @@
             out_ref[8:9, at] = jnp.sum(last, axis=0, keepdims=True)
         return carry
 
-    lax.fori_loop(0, blocks // UNROLL, fetch, 0)
+    trips = blocks // UNROLL
+    parts = 4 if trips % 4 == 0 else 1
+    copies = []
+    for part in range(parts):
+        lax.fori_loop(part * trips // parts, (part + 1) * trips // parts, fetch, 0)
+        at = pl.ds(part * blocks // parts * LANES, blocks // parts * LANES)
+        copies.append(pltpu.make_async_copy(out_ref.at[:, at], out_hbm.at[:, at], out_sem.at[part]))
+        copies[-1].start()
+    for copy in copies:
+        copy.wait()
 
 
 def return_nodes(key, first, got, windows, given_pad):
@@ -423,7 +447,8 @@
             pl.BlockSpec(memory_space=pltpu.VMEM),
             pl.BlockSpec(memory_space=pltpu.SMEM),
         ] + [pl.BlockSpec(memory_space=pltpu.VMEM)] * len(got),
-        out_specs=pl.BlockSpec(memory_space=pltpu.VMEM),
+        out_specs=pl.BlockSpec(memory_space=pltpu.HBM),
+        scratch_shapes=[pltpu.VMEM((GIVEN, blocks * LANES), jnp.float32), pltpu.SemaphoreType.DMA((4,))],
         compiler_params=pltpu.CompilerParams(vmem_limit_bytes=16 * 2**20),
         name="give_back",
     )(key, first, *got)

time: 55.9 us -> 54.1 us (0.968)
  Pallas kernels: 33.2 us -> 31.5 us
    pallas_call x1, Pallas kernels: 9.42 us -> 8.05 us  [route(): pl.pallas_call(functools.partial(route_kernel, owners, windows, patch_dev...]
  transfers between devices with their start and end apart: 7 -> 7, of which waited for: 4 -> 4; matrix products, arithmetic and copies ran while one was open for 0% -> 0% of each run, Pallas kernels for 17% -> 15%
where the time goes in v5:
time: 54.1 us; the launch traced here: 54 us
  Pallas kernels  31.5 us (58%)
  waiting for transfers between devices  14.3 us (26%)
  starting transfers between devices  8.1 us (15%)
    pallas_call x1, Pallas kernels, project_nodes(): pl.pallas_call(functools.partial(project_kernel, pairs, windows, given_pa...  17.9 us
    ppermute x7, waiting for transfers between devices, swap(): lax.ppermute(value, 'bulk', [(i, i ^ distance) for i in range(owners)])  14.3 us
    ppermute x7, starting transfers between devices, swap(): lax.ppermute(value, 'bulk', [(i, i ^ distance) for i in range(owners)])  8.1 us
    pallas_call x1, Pallas kernels, route(): pl.pallas_call(functools.partial(route_kernel, owners, windows, patch_dev...  8.05 us
    pallas_call x1, Pallas kernels, return_nodes(): pl.pallas_call(functools.partial(return_kernel, owners, windows, given_pa...  5.55 us
  transfers between devices with their start and end apart: 7, of which 4 were waited for; matrix products, arithmetic and copies ran while one was open for 0% of the time, Pallas kernels for 15%

profile of v5, /device:TPU:0, one launch (start us, length us, event | category | flops | bytes accessed | tf_op | source)
XLA Modules:
  0.0 54.0 jit_solution(4651992794556022889)
XLA Ops:
  0.0 0.5 collective-permute-start.3
  0.5 8.1 %route.1 = (f32[240,128]{1,0:T(8,128)S(1)}, f32[240,128]{1,0:T(8,128)S(1)}, f32[240,128]{1,0:T(8,128)S(1)}, f32[240,128]{1,0:T(8,128)S(1)}, s32[128,128]{1,0:T(8...) custom-call(s32[128,128]{1,0:T(8,128)} %bitcast.2, s32[128,128]{1,0:T(8,128)} %bitcast.3, s32[2,16384]{1,0:T(2,128)} %grid_hbm.1, ...), custom_call_target="tpu_custom_call" | custom-call | tf_op jit(solution)/shard_map/route/pallas_call | solution.py:142
  8.5 2.6 %collective-permute-start = (f32[240,128]{1,0:T(8,128)S(1)}, f32[240,128]{1,0:T(8,128)S(1)}, u32[]{:S(2)}, u32[]{:S(2)}) collective-permute-start(f32[240,128]{1,0:T(8,128)S(1)} %get-tuple-element.19), channel_id=1, source_target_pairs={{0,2},{1,3},{2,0},{3,1},{4,6},{5,7},{6,4},{7,5},{8,10},{9,11},{10,... | collective-permute-start | bytes 368648 | tf_op jit(solution)/shard_map/ppermute | solution.py:462
  11.1 1.5 %collective-permute-start.1 = (f32[240,128]{1,0:T(8,128)S(1)}, f32[240,128]{1,0:T(8,128)S(1)}, u32[]{:S(2)}, u32[]{:S(2)}) collective-permute-start(f32[240,128]{1,0:T(8,128)S(1)} %get-tuple-element.20), channel_id=1, source_target_pairs={{0,4},{1,5},{2,6},{3,7},{4,0},{5,1},{6,2},{7,3},{8,12},{9,13},{10,... | collective-permute-start | bytes 368648 | tf_op jit(solution)/shard_map/ppermute | solution.py:462
  12.6 0.0 collective-permute-start.2
  12.6 2.5 %collective-permute-done.refs_1_ = f32[240,128]{1,0:T(8,128)S(1)} collective-permute-done((f32[240,128]{1,0:T(8,128)S(1)}, f32[240,128]{1,0:T(8,128)S(1)}, u32[]{:S(2)}, u32[]{:S(2)}) %collective-permute-start) | collective-permute-done | bytes 122912 | tf_op jit(solution)/shard_map/ppermute | solution.py:462
  15.1 4.1 %collective-permute-done.1.refs_2_ = f32[240,128]{1,0:T(8,128)S(1)} collective-permute-done((f32[240,128]{1,0:T(8,128)S(1)}, f32[240,128]{1,0:T(8,128)S(1)}, u32[]{:S(2)}, u32[]{:S(2)}) %collective-permute-start.1) | collective-permute-done | bytes 122912 | tf_op jit(solution)/shard_map/ppermute | solution.py:462
  19.2 0.0 collective-permute-done.2.refs_3_
  19.2 0.0 collective-permute-done.3.refs_5_
  19.2 17.9 %project.1 = (f32[368,128]{1,0:T(8,128)S(1)}, f32[368,128]{1,0:T(8,128)S(1)}, f32[368,128]{1,0:T(8,128)S(1)}, f32[368,128]{1,0:T(8,128)S(1)}, f32[40064,128]{1,0:T(8,128)S(1)}) custom-call(f32[240,128]{1,0:T(8,128)S(1)} %get-tuple-element.18.refs_0_, f32[240,128]{1,0:T(8,128)S(1)} %collective-permute-done.refs_1_, ...), custom_call_target="tpu_custom_call", output_to_operand_aliasing={{4}: (4, {})} | custom-call | tf_op jit(solution)/shard_map/project/pallas_call | solution.py:373
  37.1 1.2 %collective-permute-start.4 = (f32[368,128]{1,0:T(8,128)S(1)}, f32[368,128]{1,0:T(8,128)S(1)}, u32[]{:S(2)}, u32[]{:S(2)}) collective-permute-start(f32[368,128]{1,0:T(8,128)S(1)} %get-tuple-element.24), channel_id=1, source_target_pairs={{0,2},{1,3},{2,0},{3,1},{4,6},{5,7},{6,4},{7,5},{8,10},{9,11},{10,... | collective-permute-start | bytes 565256 | tf_op jit(solution)/shard_map/ppermute | solution.py:462
  38.3 0.9 %collective-permute-start.5 = (f32[368,128]{1,0:T(8,128)S(1)}, f32[368,128]{1,0:T(8,128)S(1)}, u32[]{:S(2)}, u32[]{:S(2)}) collective-permute-start(f32[368,128]{1,0:T(8,128)S(1)} %get-tuple-element.25), channel_id=1, source_target_pairs={{0,4},{1,5},{2,6},{3,7},{4,0},{5,1},{6,2},{7,3},{8,12},{9,13},{10,... | collective-permute-start | bytes 565256 | tf_op jit(solution)/shard_map/ppermute | solution.py:462
  39.1 1.5 %collective-permute-start.6 = (f32[368,128]{1,0:T(8,128)S(1)}, f32[368,128]{1,0:T(8,128)S(1)}, u32[]{:S(2)}, u32[]{:S(2)}) collective-permute-start(f32[368,128]{1,0:T(8,128)S(1)} %get-tuple-element.26), channel_id=1, source_target_pairs={{0,6},{1,7},{2,4},{3,5},{4,2},{5,3},{6,0},{7,1},{8,14},{9,15},{10,... | collective-permute-start | bytes 565256 | tf_op jit(solution)/shard_map/ppermute | solution.py:462
  40.6 3.7 %collective-permute-done.4.refs_1_ = f32[368,128]{1,0:T(8,128)S(1)} collective-permute-done((f32[368,128]{1,0:T(8,128)S(1)}, f32[368,128]{1,0:T(8,128)S(1)}, u32[]{:S(2)}, u32[]{:S(2)}) %collective-permute-start.4) | collective-permute-done | bytes 188448 | tf_op jit(solution)/shard_map/ppermute | solution.py:462
  44.3 4.1 %collective-permute-done.5.refs_2_ = f32[368,128]{1,0:T(8,128)S(1)} collective-permute-done((f32[368,128]{1,0:T(8,128)S(1)}, f32[368,128]{1,0:T(8,128)S(1)}, u32[]{:S(2)}, u32[]{:S(2)}) %collective-permute-start.5) | collective-permute-done | bytes 188448 | tf_op jit(solution)/shard_map/ppermute | solution.py:462
  48.4 0.0 collective-permute-done.6.refs_3_
  48.4 5.6 %give_back.1 = f32[9,16384]{1,0:T(8,128)} custom-call(s32[128,128]{1,0:T(8,128)S(1)} %get-tuple-element.16.key_ref, s32[8,128]{1,0:T(8,128)S(1)} %get-tuple-element.17.first_smem, f32[368,128]{1,0:T(8,128)S(1)} %get-tuple-element.23.refs_0_, f32[368,128]{1,0:T(8,128)S(1)} %collective-permute-done.4.refs_1_, f32[368,128]{1,0:T(8,128)S(1)} %collective-permute-done.5.refs_2_, ...), custom_call_target="tpu_custom_call" | custom-call | tf_op jit(solution)/shard_map/give_back/pallas_call | solution.py:443
Async XLA Ops:
  0.0 19.2 %collective-permute-start.3 = (f32[2500,1024]{1,0:T(8,128)}, f32[2500,1024]{1,0:T(8,128)S(1)}, u32[]{:S(2)}, u32[]{:S(2)}) collective-permute-start(f32[2500,1024]{1,0:T(8,128)} %net_hbm.1), channel_id=1, source_target_pairs={{0,1},{1,0},{2,3},{3,2},{4,5},{5,4},{6,7},{7,6},{8,9},{9,8},{10,11... | collective-permute-start | bytes 30720008 | tf_op jit(solution)/shard_map/ppermute | solution.py:462
  8.5 6.5 %collective-permute-start = (f32[240,128]{1,0:T(8,128)S(1)}, f32[240,128]{1,0:T(8,128)S(1)}, u32[]{:S(2)}, u32[]{:S(2)}) collective-permute-start(f32[240,128]{1,0:T(8,128)S(1)} %get-tuple-element.19), channel_id=1, source_target_pairs={{0,2},{1,3},{2,0},{3,1},{4,6},{5,7},{6,4},{7,5},{8,10},{9,11},{10,... | collective-permute-start | bytes 368648 | tf_op jit(solution)/shard_map/ppermute | solution.py:462
  11.1 8.1 %collective-permute-start.1 = (f32[240,128]{1,0:T(8,128)S(1)}, f32[240,128]{1,0:T(8,128)S(1)}, u32[]{:S(2)}, u32[]{:S(2)}) collective-permute-start(f32[240,128]{1,0:T(8,128)S(1)} %get-tuple-element.20), channel_id=1, source_target_pairs={{0,4},{1,5},{2,6},{3,7},{4,0},{5,1},{6,2},{7,3},{8,12},{9,13},{10,... | collective-permute-start | bytes 368648 | tf_op jit(solution)/shard_map/ppermute | solution.py:462
  12.6 6.6 %collective-permute-start.2 = (f32[240,128]{1,0:T(8,128)S(1)}, f32[240,128]{1,0:T(8,128)S(1)}, u32[]{:S(2)}, u32[]{:S(2)}) collective-permute-start(f32[240,128]{1,0:T(8,128)S(1)} %get-tuple-element.21), channel_id=1, source_target_pairs={{0,6},{1,7},{2,4},{3,5},{4,2},{5,3},{6,0},{7,1},{8,14},{9,15},{10,... | collective-permute-start | bytes 368648 | tf_op jit(solution)/shard_map/ppermute | solution.py:462
  37.1 7.3 %collective-permute-start.4 = (f32[368,128]{1,0:T(8,128)S(1)}, f32[368,128]{1,0:T(8,128)S(1)}, u32[]{:S(2)}, u32[]{:S(2)}) collective-permute-start(f32[368,128]{1,0:T(8,128)S(1)} %get-tuple-element.24), channel_id=1, source_target_pairs={{0,2},{1,3},{2,0},{3,1},{4,6},{5,7},{6,4},{7,5},{8,10},{9,11},{10,... | collective-permute-start | bytes 565256 | tf_op jit(solution)/shard_map/ppermute | solution.py:462
  38.3 10.1 %collective-permute-start.5 = (f32[368,128]{1,0:T(8,128)S(1)}, f32[368,128]{1,0:T(8,128)S(1)}, u32[]{:S(2)}, u32[]{:S(2)}) collective-permute-start(f32[368,128]{1,0:T(8,128)S(1)} %get-tuple-element.25), channel_id=1, source_target_pairs={{0,4},{1,5},{2,6},{3,7},{4,0},{5,1},{6,2},{7,3},{8,12},{9,13},{10,... | collective-permute-start | bytes 565256 | tf_op jit(solution)/shard_map/ppermute | solution.py:462
  39.1 9.3 %collective-permute-start.6 = (f32[368,128]{1,0:T(8,128)S(1)}, f32[368,128]{1,0:T(8,128)S(1)}, u32[]{:S(2)}, u32[]{:S(2)}) collective-permute-start(f32[368,128]{1,0:T(8,128)S(1)} %get-tuple-element.26), channel_id=1, source_target_pairs={{0,6},{1,7},{2,4},{3,5},{4,2},{5,3},{6,0},{7,1},{8,14},{9,15},{10,... | collective-permute-start | bytes 565256 | tf_op jit(solution)/shard_map/ppermute | solution.py:462

commit v6 on v5

--- a/solution.py
+++ b/solution.py
@@ -13,7 +13,7 @@
 LANES = 128
 SENT = 6
 GIVEN = 9
-UNROLL = 16
+UNROLL = 32
 
 damping = 0.1
 
@@ -34,7 +34,7 @@
                  *refs):
     sent_refs = refs[:owners // 2]
     (key_ref, first_ref, net_ref, patch_ref, span_ref, grid_ref, target_ref,
-     code_ref, load_ref, slot_ref, first_smem, in_sem, net_sem, first_sem) = refs[owners // 2:]
+     code_ref, load_ref, slot_ref, base_ref, base_smem, in_sem, net_sem, base_sem) = refs[owners // 2:]
     me = lax.axis_index("bulk")
     copies = []
     for k, (source, to) in enumerate(
@@ -76,12 +76,14 @@
         total = counts[:, LANES:]
         offset = jnp.dot(earlier, total.astype(jnp.bfloat16), preferred_element_type=jnp.float32)
         first = jnp.sum(jnp.where(diagonal, offset, 0.0), axis=0, keepdims=True)
-        first_ref[x:x + 1, :] = first.astype(jnp.int32) >> 7
+        first = first.astype(jnp.int32) >> 7
+        first_ref[x:x + 1, :] = first
+        base_ref[x:x + 1, :] = (first + x * (windows + 1)) * 8
         before = counts[:, :LANES].astype(jnp.int32) - mine.astype(jnp.int32)
         edge = offset.astype(jnp.int32) & (LANES - 1)
         key = jnp.where(mine, before + edge + 2 * LANES * x, key)
         found.append((mine, before, edge, total.astype(jnp.int32)))
-    copy = pltpu.make_async_copy(first_ref, first_smem, first_sem)
+    copy = pltpu.make_async_copy(base_ref, base_smem, base_sem)
     copy.start()
     for load in loads[chunks // 2:]:
         load.start()
@@ -95,13 +97,13 @@
         rank = (blane - edge) & (LANES - 1)
         source = take_lanes(word & (LANES - 1), rank)
         valid = rank < total
-        code_ref[x * blocks:(x + 1) * blocks, :] = source + jnp.where(valid, jnp.where(blane >= edge, 128, 256), 0)
+        code_ref[x * blocks:(x + 1) * blocks, :] = source + jnp.where(valid, jnp.where(blane >= edge, LANES, -LANES), 0)
 
     key_ref[...] = key
     for waiting in copies[1:]:
         waiting.wait()
     span = span_ref[...]
-    row = (2 * ((span >> 1) * patch_pad + local) + (span & 1)).astype(jnp.float32)
+    row = (2 * ((span >> 1) * patch_pad + local) + (span & 1) + 1).astype(jnp.float32)
     for b in range(blocks):
         load_ref[8 * b:8 * b + 3, :] = target_ref[:, b * LANES:(b + 1) * LANES]
         load_ref[8 * b + 3:8 * b + 5, :] = (grid_ref[:, b * LANES:(b + 1) * LANES].astype(jnp.float32) + 0.5) * (1.0 / LEVELS)
@@ -115,9 +117,9 @@
             for o in range(owners):
                 code = jnp.broadcast_to(code_ref[pl.ds(o * blocks + b, 1), :], (8, LANES))
                 moved = take_lanes(load, code & (LANES - 1))
-                base = pl.multiple_of((o * (windows + 1) + first_smem[o, b]) * 8, 8)
-                pltpu.store(slot_ref.at[pl.ds(base, 8), :], moved, mask=(code & 128) != 0)
-                pltpu.store(slot_ref.at[pl.ds(base + 8, 8), :], moved, mask=(code & 256) != 0)
+                base = pl.multiple_of(base_smem[o, b], 8)
+                pltpu.store(slot_ref.at[pl.ds(base, 8), :], moved, mask=code >= LANES)
+                pltpu.store(slot_ref.at[pl.ds(base + 8, 8), :], moved, mask=code < 0)
         return carry
 
     lax.fori_loop(0, blocks // UNROLL, place, 0)
@@ -157,6 +159,7 @@
             pltpu.VMEM((owners * blocks, LANES), jnp.int32),
             pltpu.VMEM((8 * blocks, LANES), jnp.float32),
             pltpu.VMEM((owners * (windows + 1) * 8, LANES), jnp.float32),
+            pltpu.VMEM((owners, blocks), jnp.int32),
             pltpu.SMEM((owners, blocks), jnp.int32),
             pltpu.SemaphoreType.DMA((4,)),
             pltpu.SemaphoreType.DMA((chunks,)),
@@ -276,7 +279,7 @@
 
     def solve(t, k):
         turned = turns[k % 2]
-        odd = (arrived(t, SENT - 1).astype(jnp.int32) & 1) == 1
+        odd = (arrived(t, SENT - 1).astype(jnp.int32) & 1) == 0
         kept = set()
 
         def read(e):
@@ -324,7 +327,7 @@
 
     for t in range(total):
         collect(t, SENT - 1)
-        index_ref[8 * t:8 * t + 8, :] = (arrived(t, SENT - 1).astype(jnp.int32) >> 1) + t // half * rows
+        index_ref[8 * t:8 * t + 8, :] = (jnp.maximum(arrived(t, SENT - 1).astype(jnp.int32) - 1, 0) >> 1) + t // half * rows
         if t < depth:
             fetch(t, t).start()
     for c in range(chunks):
@@ -354,14 +357,26 @@
         return carry
 
     lax.fori_loop(0, total // depth - 1, steps, 0)
-    for t in range(total - depth, total):
-        if t + 2 < total:
-            fetch(t + 2, t + 2).wait()
-            interleave(gathering(t + 2), turning(t + 1), solving(t, t))
-        elif t + 1 < total:
-            interleave(turning(t + 1), solving(t, t))
-        else:
-            interleave(solving(t, t))
+    used = jnp.max(jnp.maximum(arrived(total - 2, SENT - 1), arrived(total - 1, SENT - 1))) > 0.0
+
+    @pl.when(used)
+    def _():
+        for t in range(total - depth, total):
+            if t + 2 < total:
+                fetch(t + 2, t + 2).wait()
+                interleave(gathering(t + 2), turning(t + 1), solving(t, t))
+            elif t + 1 < total:
+                interleave(turning(t + 1), solving(t, t))
+            else:
+                interleave(solving(t, t))
+
+    @pl.when(jnp.logical_not(used))
+    def _():
+        for t in (total - 2, total - 1):
+            fetch(t, t).wait()
+        interleave(turning(total - 3), solving(total - 4, total - 4))
+        interleave(solving(total - 3, total - 3))
+
     for t in (total, total + 1):
         fetch(t, t).wait()
 

time: 54.1 us -> 53.2 us (0.983)
  Pallas kernels: 31.5 us -> 29.4 us
  starting transfers between devices: 8.1 us -> 9.04 us
    pallas_call x1, Pallas kernels: 17.9 us -> 16.5 us  [project_nodes(): pl.pallas_call(functools.partial(project_kernel, pairs, windows, given_pa...]
    ppermute x7, starting transfers between devices: 8.1 us -> 9.04 us  [swap(): lax.ppermute(value, 'bulk', [(i, i ^ distance) for i in range(owners)])]
where the time goes in v6:
time: 53.2 us; the launch traced here: 52.7 us
  Pallas kernels  29.4 us (55%)
  waiting for transfers between devices  14.1 us (27%)
  starting transfers between devices  9.04 us (17%)
    pallas_call x1, Pallas kernels, project_nodes(): pl.pallas_call(functools.partial(project_kernel, pairs, windows, given_pa...  16.5 us
    ppermute x7, waiting for transfers between devices, swap(): lax.ppermute(value, 'bulk', [(i, i ^ distance) for i in range(owners)])  14.1 us
    ppermute x7, starting transfers between devices, swap(): lax.ppermute(value, 'bulk', [(i, i ^ distance) for i in range(owners)])  9.04 us
    pallas_call x1, Pallas kernels, route(): pl.pallas_call(functools.partial(route_kernel, owners, windows, patch_dev...  7.77 us
    pallas_call x1, Pallas kernels, return_nodes(): pl.pallas_call(functools.partial(return_kernel, owners, windows, given_pa...  5.1 us
  transfers between devices with their start and end apart: 7, of which 4 were waited for; matrix products, arithmetic and copies ran while one was open for 0% of the time, Pallas kernels for 15%

profile of v6, /device:TPU:0, one launch (start us, length us, event | category | flops | bytes accessed | tf_op | source)
XLA Modules:
  0.0 52.7 jit_solution(8756963378463337367)
XLA Ops:
  0.0 0.5 collective-permute-start.3
  0.5 7.8 %route.1 = (f32[240,128]{1,0:T(8,128)S(1)}, f32[240,128]{1,0:T(8,128)S(1)}, f32[240,128]{1,0:T(8,128)S(1)}, f32[240,128]{1,0:T(8,128)S(1)}, s32[128,128]{1,0:T(8...) custom-call(s32[128,128]{1,0:T(8,128)} %bitcast.2, s32[128,128]{1,0:T(8,128)} %bitcast.3, s32[2,16384]{1,0:T(2,128)} %grid_hbm.1, ...), custom_call_target="tpu_custom_call" | custom-call | tf_op jit(solution)/shard_map/route/pallas_call | solution.py:144
  8.2 2.6 %collective-permute-start = (f32[240,128]{1,0:T(8,128)S(1)}, f32[240,128]{1,0:T(8,128)S(1)}, u32[]{:S(2)}, u32[]{:S(2)}) collective-permute-start(f32[240,128]{1,0:T(8,128)S(1)} %get-tuple-element.19), channel_id=1, source_target_pairs={{0,2},{1,3},{2,0},{3,1},{4,6},{5,7},{6,4},{7,5},{8,10},{9,11},{10,... | collective-permute-start | bytes 368648 | tf_op jit(solution)/shard_map/ppermute | solution.py:477
  10.8 1.5 %collective-permute-start.1 = (f32[240,128]{1,0:T(8,128)S(1)}, f32[240,128]{1,0:T(8,128)S(1)}, u32[]{:S(2)}, u32[]{:S(2)}) collective-permute-start(f32[240,128]{1,0:T(8,128)S(1)} %get-tuple-element.20), channel_id=1, source_target_pairs={{0,4},{1,5},{2,6},{3,7},{4,0},{5,1},{6,2},{7,3},{8,12},{9,13},{10,... | collective-permute-start | bytes 368648 | tf_op jit(solution)/shard_map/ppermute | solution.py:477
  12.3 0.0 collective-permute-start.2
  12.3 2.5 %collective-permute-done.refs_1_ = f32[240,128]{1,0:T(8,128)S(1)} collective-permute-done((f32[240,128]{1,0:T(8,128)S(1)}, f32[240,128]{1,0:T(8,128)S(1)}, u32[]{:S(2)}, u32[]{:S(2)}) %collective-permute-start) | collective-permute-done | bytes 122912 | tf_op jit(solution)/shard_map/ppermute | solution.py:477
  14.8 4.1 %collective-permute-done.1.refs_2_ = f32[240,128]{1,0:T(8,128)S(1)} collective-permute-done((f32[240,128]{1,0:T(8,128)S(1)}, f32[240,128]{1,0:T(8,128)S(1)}, u32[]{:S(2)}, u32[]{:S(2)}) %collective-permute-start.1) | collective-permute-done | bytes 122912 | tf_op jit(solution)/shard_map/ppermute | solution.py:477
  18.9 0.0 collective-permute-done.2.refs_3_
  18.9 0.0 collective-permute-done.3.refs_5_
  18.9 16.5 %project.1 = (f32[368,128]{1,0:T(8,128)S(1)}, f32[368,128]{1,0:T(8,128)S(1)}, f32[368,128]{1,0:T(8,128)S(1)}, f32[368,128]{1,0:T(8,128)S(1)}, f32[40064,128]{1,0:T(8,128)S(1)}) custom-call(f32[240,128]{1,0:T(8,128)S(1)} %get-tuple-element.18.refs_0_, f32[240,128]{1,0:T(8,128)S(1)} %collective-permute-done.refs_1_, ...), custom_call_target="tpu_custom_call", output_to_operand_aliasing={{4}: (4, {})} | custom-call | tf_op jit(solution)/shard_map/project/pallas_call | solution.py:388
  35.4 2.9 %collective-permute-start.4 = (f32[368,128]{1,0:T(8,128)S(1)}, f32[368,128]{1,0:T(8,128)S(1)}, u32[]{:S(2)}, u32[]{:S(2)}) collective-permute-start(f32[368,128]{1,0:T(8,128)S(1)} %get-tuple-element.24), channel_id=1, source_target_pairs={{0,2},{1,3},{2,0},{3,1},{4,6},{5,7},{6,4},{7,5},{8,10},{9,11},{10,... | collective-permute-start | bytes 565256 | tf_op jit(solution)/shard_map/ppermute | solution.py:477
  38.4 0.0 collective-permute-start.5
  38.4 1.5 %collective-permute-start.6 = (f32[368,128]{1,0:T(8,128)S(1)}, f32[368,128]{1,0:T(8,128)S(1)}, u32[]{:S(2)}, u32[]{:S(2)}) collective-permute-start(f32[368,128]{1,0:T(8,128)S(1)} %get-tuple-element.26), channel_id=1, source_target_pairs={{0,6},{1,7},{2,4},{3,5},{4,2},{5,3},{6,0},{7,1},{8,14},{9,15},{10,... | collective-permute-start | bytes 565256 | tf_op jit(solution)/shard_map/ppermute | solution.py:477
  39.9 4.0 %collective-permute-done.4.refs_1_ = f32[368,128]{1,0:T(8,128)S(1)} collective-permute-done((f32[368,128]{1,0:T(8,128)S(1)}, f32[368,128]{1,0:T(8,128)S(1)}, u32[]{:S(2)}, u32[]{:S(2)}) %collective-permute-start.4) | collective-permute-done | bytes 188448 | tf_op jit(solution)/shard_map/ppermute | solution.py:477
  43.9 3.6 %collective-permute-done.5.refs_2_ = f32[368,128]{1,0:T(8,128)S(1)} collective-permute-done((f32[368,128]{1,0:T(8,128)S(1)}, f32[368,128]{1,0:T(8,128)S(1)}, u32[]{:S(2)}, u32[]{:S(2)}) %collective-permute-start.5) | collective-permute-done | bytes 188448 | tf_op jit(solution)/shard_map/ppermute | solution.py:477
  47.5 0.0 collective-permute-done.6.refs_3_
  47.5 5.1 %give_back.1 = f32[9,16384]{1,0:T(8,128)} custom-call(s32[128,128]{1,0:T(8,128)S(1)} %get-tuple-element.16.key_ref, s32[8,128]{1,0:T(8,128)S(1)} %get-tuple-element.17.first_smem, f32[368,128]{1,0:T(8,128)S(1)} %get-tuple-element.23.refs_0_, f32[368,128]{1,0:T(8,128)S(1)} %collective-permute-done.4.refs_1_, f32[368,128]{1,0:T(8,128)S(1)} %collective-permute-done.5.refs_2_, ...), custom_call_target="tpu_custom_call" | custom-call | tf_op jit(solution)/shard_map/give_back/pallas_call | solution.py:458
Async XLA Ops:
  0.0 18.9 %collective-permute-start.3 = (f32[2500,1024]{1,0:T(8,128)}, f32[2500,1024]{1,0:T(8,128)S(1)}, u32[]{:S(2)}, u32[]{:S(2)}) collective-permute-start(f32[2500,1024]{1,0:T(8,128)} %net_hbm.1), channel_id=1, source_target_pairs={{0,1},{1,0},{2,3},{3,2},{4,5},{5,4},{6,7},{7,6},{8,9},{9,8},{10,11... | collective-permute-start | bytes 30720008 | tf_op jit(solution)/shard_map/ppermute | solution.py:477
  8.2 6.5 %collective-permute-start = (f32[240,128]{1,0:T(8,128)S(1)}, f32[240,128]{1,0:T(8,128)S(1)}, u32[]{:S(2)}, u32[]{:S(2)}) collective-permute-start(f32[240,128]{1,0:T(8,128)S(1)} %get-tuple-element.19), channel_id=1, source_target_pairs={{0,2},{1,3},{2,0},{3,1},{4,6},{5,7},{6,4},{7,5},{8,10},{9,11},{10,... | collective-permute-start | bytes 368648 | tf_op jit(solution)/shard_map/ppermute | solution.py:477
  10.8 8.1 %collective-permute-start.1 = (f32[240,128]{1,0:T(8,128)S(1)}, f32[240,128]{1,0:T(8,128)S(1)}, u32[]{:S(2)}, u32[]{:S(2)}) collective-permute-start(f32[240,128]{1,0:T(8,128)S(1)} %get-tuple-element.20), channel_id=1, source_target_pairs={{0,4},{1,5},{2,6},{3,7},{4,0},{5,1},{6,2},{7,3},{8,12},{9,13},{10,... | collective-permute-start | bytes 368648 | tf_op jit(solution)/shard_map/ppermute | solution.py:477
  12.3 6.6 %collective-permute-start.2 = (f32[240,128]{1,0:T(8,128)S(1)}, f32[240,128]{1,0:T(8,128)S(1)}, u32[]{:S(2)}, u32[]{:S(2)}) collective-permute-start(f32[240,128]{1,0:T(8,128)S(1)} %get-tuple-element.21), channel_id=1, source_target_pairs={{0,6},{1,7},{2,4},{3,5},{4,2},{5,3},{6,0},{7,1},{8,14},{9,15},{10,... | collective-permute-start | bytes 368648 | tf_op jit(solution)/shard_map/ppermute | solution.py:477
  35.4 8.5 %collective-permute-start.4 = (f32[368,128]{1,0:T(8,128)S(1)}, f32[368,128]{1,0:T(8,128)S(1)}, u32[]{:S(2)}, u32[]{:S(2)}) collective-permute-start(f32[368,128]{1,0:T(8,128)S(1)} %get-tuple-element.24), channel_id=1, source_target_pairs={{0,2},{1,3},{2,0},{3,1},{4,6},{5,7},{6,4},{7,5},{8,10},{9,11},{10,... | collective-permute-start | bytes 565256 | tf_op jit(solution)/shard_map/ppermute | solution.py:477
  38.4 9.1 %collective-permute-start.5 = (f32[368,128]{1,0:T(8,128)S(1)}, f32[368,128]{1,0:T(8,128)S(1)}, u32[]{:S(2)}, u32[]{:S(2)}) collective-permute-start(f32[368,128]{1,0:T(8,128)S(1)} %get-tuple-element.25), channel_id=1, source_target_pairs={{0,4},{1,5},{2,6},{3,7},{4,0},{5,1},{6,2},{7,3},{8,12},{9,13},{10,... | collective-permute-start | bytes 565256 | tf_op jit(solution)/shard_map/ppermute | solution.py:477
  38.4 9.1 %collective-permute-start.6 = (f32[368,128]{1,0:T(8,128)S(1)}, f32[368,128]{1,0:T(8,128)S(1)}, u32[]{:S(2)}, u32[]{:S(2)}) collective-permute-start(f32[368,128]{1,0:T(8,128)S(1)} %get-tuple-element.26), channel_id=1, source_target_pairs={{0,6},{1,7},{2,4},{3,5},{4,2},{5,3},{6,0},{7,1},{8,14},{9,15},{10,... | collective-permute-start | bytes 565256 | tf_op jit(solution)/shard_map/ppermute | solution.py:477

commit v7 on v6

--- a/solution.py
+++ b/solution.py
@@ -290,7 +290,7 @@
             return coeff_ref[at, :]
 
         def finish(result):
-            base = t // half * given_pad + t % half * per
+            base = owner_of(t) * given_pad + t % half * per
             for c in range(GIVEN):
                 at = (c + 1) % GIVEN
                 for j in range(pairs):
@@ -319,15 +319,24 @@
     def solving(t, k):
         return solve(t, k), PROJECT_STEPS
 
+    at = SENT * windows - 2 * per
+    tail = got_refs[0][at:at + 2 * per, :]
+    for j in range(1, pairs):
+        tail = jnp.maximum(tail, got_refs[j][at:at + 2 * per, :])
+    turned_round = jnp.where(jnp.max(tail) > 0.0, 0, 1)
+
+    def owner_of(t):
+        return t // half ^ turned_round
+
     def collect(t, c):
-        at = (t // half * SENT + c) * windows + t % half * per
+        at = (owner_of(t) * SENT + c) * windows + t % half * per
         for j in range(pairs):
             to = (t * SENT + c) * 8 + j * per
-            load_ref[to:to + per, :] = got_refs[j][at:at + per, :]
+            load_ref[to:to + per, :] = got_refs[j][pl.ds(at, per), :]
 
     for t in range(total):
         collect(t, SENT - 1)
-        index_ref[8 * t:8 * t + 8, :] = (jnp.maximum(arrived(t, SENT - 1).astype(jnp.int32) - 1, 0) >> 1) + t // half * rows
+        index_ref[8 * t:8 * t + 8, :] = (jnp.maximum(arrived(t, SENT - 1).astype(jnp.int32) - 1, 0) >> 1) + owner_of(t) * rows
         if t < depth:
             fetch(t, t).start()
     for c in range(chunks):
@@ -335,6 +344,8 @@
     for t in range(total):
         for c in range(SENT - 1):
             collect(t, c)
+    for c in range(chunks):
+        partner(c).wait()
     index_ref[8 * total:8 * total + 16, :] = jnp.zeros((16, LANES), jnp.int32)
     fetch(0, 0).wait()
     interleave(gathering(0))
@@ -344,11 +355,6 @@
     fetch(depth + 1, depth + 1).start()
 
     def steps(i, carry):
-        @pl.when(i == -(-(half - depth - 1) // depth))
-        def _():
-            for c in range(chunks):
-                partner(c).wait()
-
         for k in range(depth):
             t = depth * i + k
             fetch(t + 2, k + 2).wait()

time: 53.2 us -> 52.3 us (0.983)
  starting transfers between devices: 9.04 us -> 8.1 us
    ppermute x7, starting transfers between devices: 9.04 us -> 8.1 us  [swap(): lax.ppermute(value, 'bulk', [(i, i ^ distance) for i in range(owners)])]
where the time goes in v7:
time: 52.3 us; the launch traced here: 52.2 us
  Pallas kernels  29.5 us (56%)
  waiting for transfers between devices  14.4 us (28%)
  starting transfers between devices  8.1 us (15%)
    pallas_call x1, Pallas kernels, project_nodes(): pl.pallas_call(functools.partial(project_kernel, pairs, windows, given_pa...  16.7 us
    ppermute x7, waiting for transfers between devices, swap(): lax.ppermute(value, 'bulk', [(i, i ^ distance) for i in range(owners)])  14.4 us
    ppermute x7, starting transfers between devices, swap(): lax.ppermute(value, 'bulk', [(i, i ^ distance) for i in range(owners)])  8.1 us
    pallas_call x1, Pallas kernels, route(): pl.pallas_call(functools.partial(route_kernel, owners, windows, patch_dev...  7.77 us
    pallas_call x1, Pallas kernels, return_nodes(): pl.pallas_call(functools.partial(return_kernel, owners, windows, given_pa...  5.08 us
  transfers between devices with their start and end apart: 7, of which 4 were waited for; matrix products, arithmetic and copies ran while one was open for 0% of the time, Pallas kernels for 15%

profile of v7, /device:TPU:0, one launch (start us, length us, event | category | flops | bytes accessed | tf_op | source)
XLA Modules:
  0.0 52.2 jit_solution(2480858215289031907)
XLA Ops:
  0.0 0.5 collective-permute-start.3
  0.5 7.8 %route.1 = (f32[240,128]{1,0:T(8,128)S(1)}, f32[240,128]{1,0:T(8,128)S(1)}, f32[240,128]{1,0:T(8,128)S(1)}, f32[240,128]{1,0:T(8,128)S(1)}, s32[128,128]{1,0:T(8...) custom-call(s32[128,128]{1,0:T(8,128)} %bitcast.2, s32[128,128]{1,0:T(8,128)} %bitcast.3, s32[2,16384]{1,0:T(2,128)} %grid_hbm.1, ...), custom_call_target="tpu_custom_call" | custom-call | tf_op jit(solution)/shard_map/route/pallas_call | solution.py:144
  8.2 2.6 %collective-permute-start = (f32[240,128]{1,0:T(8,128)S(1)}, f32[240,128]{1,0:T(8,128)S(1)}, u32[]{:S(2)}, u32[]{:S(2)}) collective-permute-start(f32[240,128]{1,0:T(8,128)S(1)} %get-tuple-element.19), channel_id=1, source_target_pairs={{0,2},{1,3},{2,0},{3,1},{4,6},{5,7},{6,4},{7,5},{8,10},{9,11},{10,... | collective-permute-start | bytes 368648 | tf_op jit(solution)/shard_map/ppermute | solution.py:483
  10.8 1.5 %collective-permute-start.1 = (f32[240,128]{1,0:T(8,128)S(1)}, f32[240,128]{1,0:T(8,128)S(1)}, u32[]{:S(2)}, u32[]{:S(2)}) collective-permute-start(f32[240,128]{1,0:T(8,128)S(1)} %get-tuple-element.20), channel_id=1, source_target_pairs={{0,4},{1,5},{2,6},{3,7},{4,0},{5,1},{6,2},{7,3},{8,12},{9,13},{10,... | collective-permute-start | bytes 368648 | tf_op jit(solution)/shard_map/ppermute | solution.py:483
  12.3 0.0 collective-permute-start.2
  12.3 2.5 %collective-permute-done.refs_1_ = f32[240,128]{1,0:T(8,128)S(1)} collective-permute-done((f32[240,128]{1,0:T(8,128)S(1)}, f32[240,128]{1,0:T(8,128)S(1)}, u32[]{:S(2)}, u32[]{:S(2)}) %collective-permute-start) | collective-permute-done | bytes 122912 | tf_op jit(solution)/shard_map/ppermute | solution.py:483
  14.8 4.1 %collective-permute-done.1.refs_2_ = f32[240,128]{1,0:T(8,128)S(1)} collective-permute-done((f32[240,128]{1,0:T(8,128)S(1)}, f32[240,128]{1,0:T(8,128)S(1)}, u32[]{:S(2)}, u32[]{:S(2)}) %collective-permute-start.1) | collective-permute-done | bytes 122912 | tf_op jit(solution)/shard_map/ppermute | solution.py:483
  18.9 0.0 collective-permute-done.2.refs_3_
  18.9 0.0 collective-permute-done.3.refs_5_
  18.9 16.7 %project.1 = (f32[368,128]{1,0:T(8,128)S(1)}, f32[368,128]{1,0:T(8,128)S(1)}, f32[368,128]{1,0:T(8,128)S(1)}, f32[368,128]{1,0:T(8,128)S(1)}, f32[40064,128]{1,0:T(8,128)S(1)}) custom-call(f32[240,128]{1,0:T(8,128)S(1)} %get-tuple-element.18.refs_0_, f32[240,128]{1,0:T(8,128)S(1)} %collective-permute-done.refs_1_, ...), custom_call_target="tpu_custom_call", output_to_operand_aliasing={{4}: (4, {})} | custom-call | tf_op jit(solution)/shard_map/project/pallas_call | solution.py:394
  35.6 1.3 %collective-permute-start.4 = (f32[368,128]{1,0:T(8,128)S(1)}, f32[368,128]{1,0:T(8,128)S(1)}, u32[]{:S(2)}, u32[]{:S(2)}) collective-permute-start(f32[368,128]{1,0:T(8,128)S(1)} %get-tuple-element.24), channel_id=1, source_target_pairs={{0,2},{1,3},{2,0},{3,1},{4,6},{5,7},{6,4},{7,5},{8,10},{9,11},{10,... | collective-permute-start | bytes 565256 | tf_op jit(solution)/shard_map/ppermute | solution.py:483
  36.8 0.8 %collective-permute-start.5 = (f32[368,128]{1,0:T(8,128)S(1)}, f32[368,128]{1,0:T(8,128)S(1)}, u32[]{:S(2)}, u32[]{:S(2)}) collective-permute-start(f32[368,128]{1,0:T(8,128)S(1)} %get-tuple-element.25), channel_id=1, source_target_pairs={{0,4},{1,5},{2,6},{3,7},{4,0},{5,1},{6,2},{7,3},{8,12},{9,13},{10,... | collective-permute-start | bytes 565256 | tf_op jit(solution)/shard_map/ppermute | solution.py:483
  37.6 1.5 %collective-permute-start.6 = (f32[368,128]{1,0:T(8,128)S(1)}, f32[368,128]{1,0:T(8,128)S(1)}, u32[]{:S(2)}, u32[]{:S(2)}) collective-permute-start(f32[368,128]{1,0:T(8,128)S(1)} %get-tuple-element.26), channel_id=1, source_target_pairs={{0,6},{1,7},{2,4},{3,5},{4,2},{5,3},{6,0},{7,1},{8,14},{9,15},{10,... | collective-permute-start | bytes 565256 | tf_op jit(solution)/shard_map/ppermute | solution.py:483
  39.1 3.8 %collective-permute-done.4.refs_1_ = f32[368,128]{1,0:T(8,128)S(1)} collective-permute-done((f32[368,128]{1,0:T(8,128)S(1)}, f32[368,128]{1,0:T(8,128)S(1)}, u32[]{:S(2)}, u32[]{:S(2)}) %collective-permute-start.4) | collective-permute-done | bytes 188448 | tf_op jit(solution)/shard_map/ppermute | solution.py:483
  42.9 4.1 %collective-permute-done.5.refs_2_ = f32[368,128]{1,0:T(8,128)S(1)} collective-permute-done((f32[368,128]{1,0:T(8,128)S(1)}, f32[368,128]{1,0:T(8,128)S(1)}, u32[]{:S(2)}, u32[]{:S(2)}) %collective-permute-start.5) | collective-permute-done | bytes 188448 | tf_op jit(solution)/shard_map/ppermute | solution.py:483
  47.0 0.0 collective-permute-done.6.refs_3_
  47.0 5.1 %give_back.1 = f32[9,16384]{1,0:T(8,128)} custom-call(s32[128,128]{1,0:T(8,128)S(1)} %get-tuple-element.16.key_ref, s32[8,128]{1,0:T(8,128)S(1)} %get-tuple-element.17.first_smem, f32[368,128]{1,0:T(8,128)S(1)} %get-tuple-element.23.refs_0_, f32[368,128]{1,0:T(8,128)S(1)} %collective-permute-done.4.refs_1_, f32[368,128]{1,0:T(8,128)S(1)} %collective-permute-done.5.refs_2_, ...), custom_call_target="tpu_custom_call" | custom-call | tf_op jit(solution)/shard_map/give_back/pallas_call | solution.py:464
Async XLA Ops:
  0.0 18.9 %collective-permute-start.3 = (f32[2500,1024]{1,0:T(8,128)}, f32[2500,1024]{1,0:T(8,128)S(1)}, u32[]{:S(2)}, u32[]{:S(2)}) collective-permute-start(f32[2500,1024]{1,0:T(8,128)} %net_hbm.1), channel_id=1, source_target_pairs={{0,1},{1,0},{2,3},{3,2},{4,5},{5,4},{6,7},{7,6},{8,9},{9,8},{10,11... | collective-permute-start | bytes 30720008 | tf_op jit(solution)/shard_map/ppermute | solution.py:483
  8.2 6.5 %collective-permute-start = (f32[240,128]{1,0:T(8,128)S(1)}, f32[240,128]{1,0:T(8,128)S(1)}, u32[]{:S(2)}, u32[]{:S(2)}) collective-permute-start(f32[240,128]{1,0:T(8,128)S(1)} %get-tuple-element.19), channel_id=1, source_target_pairs={{0,2},{1,3},{2,0},{3,1},{4,6},{5,7},{6,4},{7,5},{8,10},{9,11},{10,... | collective-permute-start | bytes 368648 | tf_op jit(solution)/shard_map/ppermute | solution.py:483
  10.8 8.1 %collective-permute-start.1 = (f32[240,128]{1,0:T(8,128)S(1)}, f32[240,128]{1,0:T(8,128)S(1)}, u32[]{:S(2)}, u32[]{:S(2)}) collective-permute-start(f32[240,128]{1,0:T(8,128)S(1)} %get-tuple-element.20), channel_id=1, source_target_pairs={{0,4},{1,5},{2,6},{3,7},{4,0},{5,1},{6,2},{7,3},{8,12},{9,13},{10,... | collective-permute-start | bytes 368648 | tf_op jit(solution)/shard_map/ppermute | solution.py:483
  12.3 6.6 %collective-permute-start.2 = (f32[240,128]{1,0:T(8,128)S(1)}, f32[240,128]{1,0:T(8,128)S(1)}, u32[]{:S(2)}, u32[]{:S(2)}) collective-permute-start(f32[240,128]{1,0:T(8,128)S(1)} %get-tuple-element.21), channel_id=1, source_target_pairs={{0,6},{1,7},{2,4},{3,5},{4,2},{5,3},{6,0},{7,1},{8,14},{9,15},{10,... | collective-permute-start | bytes 368648 | tf_op jit(solution)/shard_map/ppermute | solution.py:483
  35.6 7.3 %collective-permute-start.4 = (f32[368,128]{1,0:T(8,128)S(1)}, f32[368,128]{1,0:T(8,128)S(1)}, u32[]{:S(2)}, u32[]{:S(2)}) collective-permute-start(f32[368,128]{1,0:T(8,128)S(1)} %get-tuple-element.24), channel_id=1, source_target_pairs={{0,2},{1,3},{2,0},{3,1},{4,6},{5,7},{6,4},{7,5},{8,10},{9,11},{10,... | collective-permute-start | bytes 565256 | tf_op jit(solution)/shard_map/ppermute | solution.py:483
  36.8 10.1 %collective-permute-start.5 = (f32[368,128]{1,0:T(8,128)S(1)}, f32[368,128]{1,0:T(8,128)S(1)}, u32[]{:S(2)}, u32[]{:S(2)}) collective-permute-start(f32[368,128]{1,0:T(8,128)S(1)} %get-tuple-element.25), channel_id=1, source_target_pairs={{0,4},{1,5},{2,6},{3,7},{4,0},{5,1},{6,2},{7,3},{8,12},{9,13},{10,... | collective-permute-start | bytes 565256 | tf_op jit(solution)/shard_map/ppermute | solution.py:483
  37.6 9.3 %collective-permute-start.6 = (f32[368,128]{1,0:T(8,128)S(1)}, f32[368,128]{1,0:T(8,128)S(1)}, u32[]{:S(2)}, u32[]{:S(2)}) collective-permute-start(f32[368,128]{1,0:T(8,128)S(1)} %get-tuple-element.26), channel_id=1, source_target_pairs={{0,6},{1,7},{2,4},{3,5},{4,2},{5,3},{6,0},{7,1},{8,14},{9,15},{10,... | collective-permute-start | bytes 565256 | tf_op jit(solution)/shard_map/ppermute | solution.py:483
